TPU v7x, 32 devices: a whole 2x2x4 slice. The times are simulated.
32 devices in a mesh: dp: 16 (over z, y, x), mp: 2 (over core).
Axes of the slice: x: 2, y: 2, z: 4, core: 2. Of those that a mesh axis runs over, the one named last changes fastest.
Arguments:
- tokens: bfloat16 [25216, 384], P('dp'), may hold values from -6 to 6
- cotangent: bfloat16 [25216, 384], P('dp'), may hold values from -6 to 6
- queue: bfloat16 [2048, 384], P('dp'), may hold values from -6 to 6
- nbr_index: int32 [128, 8], P('dp'), may hold values from 0 to 2047
- nbr_valid: int32 [128, 8], P('dp'), may hold values 0 or 1
- norm_params: float32 [4, 384], replicated, may hold values from -1 to 2.41, as said below
- norm_first: float32 [4, 384], replicated, may hold values from -160 to 160
- norm_second: float32 [4, 384], replicated, may hold values from 2773.76 to 11347.2
- attn_weight: float32 [4, 384, 384], P(None, None, 'mp'), may hold values from -0.8164966 to 0.8164966
- mlp_weight: float32 [2, 384, 1536], P(None, None, 'mp'), may hold values from -0.21875 to 0.21875
- attn_first: float32 [4, 384, 384], P(None, None, 'mp'), may hold values from -104.80501 to 104.80501
- attn_second: float32 [4, 384, 384], P(None, None, 'mp'), may hold values from 118.5152 to 11952.384
- mlp_first: float32 [2, 384, 1536], P(None, None, 'mp'), may hold values from -48 to 48
- mlp_second: float32 [2, 384, 1536], P(None, None, 'mp'), may hold values from 264.768 to 1059.072
- attn_left: float32 [4, 768, 384], P(None, 'mp'), may hold values from -0.03827328 to 1.0382733, as said below
- attn_right: float32 [4, 384, 192], P(None, 'mp'), may hold values from -0.054126588 to 1.0541266, as said below
- mlp_left: float32 [2, 768, 384], P(None, 'mp'), may hold values from -0.03827328 to 1.0382733, as said below
- mlp_right: float32 [2, 1536, 768], P(None, 'mp'), may hold values from -0.027063294 to 1.0270633, as said below
Outputs:
- block_out: bfloat16 [25216, 384], P('dp')
- input_grad: float32 [25216, 384], P('dp')
- norm_grad: float32 [4, 384], replicated
- attn_grad: float32 [4, 384, 384], P(None, None, 'mp')
- mlp_grad: float32 [2, 384, 1536], P(None, None, 'mp')
- norm_first_new: float32 [4, 384], replicated
- norm_second_new: float32 [4, 384], replicated
- norm_new: float32 [4, 384], replicated
- attn_first_new: float32 [4, 384, 384], P(None, None, 'mp')
- attn_second_new: float32 [4, 384, 384], P(None, None, 'mp')
- mlp_first_new: float32 [2, 384, 1536], P(None, None, 'mp')
- mlp_second_new: float32 [2, 384, 1536], P(None, None, 'mp')
- attn_left_new: float32 [4, 768, 384], P(None, 'mp')
- attn_right_new: float32 [4, 384, 192], P(None, 'mp')
- mlp_left_new: float32 [2, 768, 384], P(None, 'mp')
- mlp_right_new: float32 [2, 1536, 768], P(None, 'mp')
- attn_new: float32 [4, 384, 384], P(None, None, 'mp')
- attn_copy: bfloat16 [4, 384, 384], P(None, None, 'mp')
- mlp_new: float32 [2, 384, 1536], P(None, None, 'mp')
- mlp_copy: bfloat16 [2, 384, 1536], P(None, None, 'mp')
Inputs may be any that keep to these rules, and one draw needn't show every extreme that they name: `norm_params`: rows 0 and 2 are positive gains, rows 1 and 3 shifts. `attn_left`: each block of rows is a full-rank basis. `attn_right`: each block of rows is a full-rank basis. `mlp_left`: each block of rows is a full-rank basis. `mlp_right`: each block of rows is a full-rank basis.
All inputs are finite; a program needn't handle non-finite values. No bound on the sum of `nbr_valid` on one device may be relied on, other than what follows from the above.
Results may differ from a plain program's by a relative error of at most 0.0095.
The roundings to bfloat16 on the way count: a program that leaves them out, or rounds other values in their place, can miss the bound.
Values may be sent and summed in bfloat16 or wider, within the bound.
A program may use at most 256 MiB of HBM per device.

v0:
```python
import functools
import math

import jax
import jax.numpy as jnp
from jax import lax
from jax.experimental import pallas as pl
from jax.experimental.pallas import tpu as pltpu
from jax.sharding import PartitionSpec as P

BETA_FIRST = 0.9
BETA_SECOND = 0.95
EPSILON = 1e-08
RATE_MATRIX = 0.15
DECAY_RATE = 0.05
TURN_RATE = 4.0
STEP = 10
BLOCK = 256
ROUNDS = 3
NEAR = 0.01
PIECE = 128

BF = jnp.bfloat16
F32 = jnp.float32


def dot_nn(a, b):
    return lax.dot_general(a, b, (((1,), (0,)), ((), ())), preferred_element_type=F32)


def dot_nt(a, b):
    return lax.dot_general(a, b, (((1,), (1,)), ((), ())), preferred_element_type=F32)


def dot_tn(a, b):
    return lax.dot_general(a, b, (((0,), (0,)), ((), ())), preferred_element_type=F32)


def split(a):
    high = a.astype(BF)
    return high, (a - high.astype(F32)).astype(BF)


def three(dot, a, b):
    return dot(a[0], b[0]) + (dot(a[0], b[1]) + dot(a[1], b[0]))


def below(size):
    row = lax.broadcasted_iota(jnp.int32, (size, size), 0)
    col = lax.broadcasted_iota(jnp.int32, (size, size), 1)
    return row > col, row == col


def in_step(chains):
    chains = list(chains)
    while chains:
        kept = []
        for chain in chains:
            try:
                next(chain)
                kept.append(chain)
            except StopIteration:
                pass
        chains = kept


def renew_chain(base_ref, out_ref, rest_ref, misses):
    width = base_ref.shape[1]
    source = base_ref
    for at in range(0, width, BLOCK):
        size = min(BLOCK, width - at)
        lower, same = below(size)
        eye = jnp.where(same, 1.0, 0.0)
        low = source[:, at:at + size].astype(BF)
        gram = dot_tn(low, low)
        yield
        on_diag = jnp.where(same, gram, 0.0)
        s_col = lax.rsqrt(jnp.maximum(jnp.sum(on_diag, axis=1, keepdims=True), 1e-30))
        s_row = lax.rsqrt(jnp.maximum(jnp.sum(on_diag, axis=0, keepdims=True), 1e-30))
        state = gram * s_col * s_row
        made = jnp.where(same, s_col, 0.0).astype(BF)
        for turn in range(ROUNDS):
            under = jnp.where(lower, state, 0.0)
            moved = dot_nn(under.astype(BF), state.astype(BF))
            mass = jnp.sum(under * under, axis=1, keepdims=True)
            yield
            curve = jnp.sum(moved * under, axis=1, keepdims=True)
            pace = jnp.where(curve > mass, mass / jnp.maximum(curve, 1e-30), 1.0)
            left = 1.0 - 2.0 * pace * mass + pace * pace * curve
            scale = lax.rsqrt(jnp.maximum(left, 1e-6))
            step = (scale * (eye - pace * under)).astype(BF)
            if turn + 1 < ROUNDS:
                state = dot_nt((scale * (state - pace * moved)).astype(BF), step)
            made = dot_nn(step, made).astype(BF)
            yield
        high, low = split(source[:, at:at + size])
        block = dot_nt(high, made) + dot_nt(low, made)
        yield
        pair = split(block)
        gram = three(dot_tn, pair, pair)
        yield
        off = jnp.where(lower, gram, 0.0) + jnp.where(same, 0.5 * (gram - 1.0), 0.0)
        misses.append(jnp.sum(off * off) * (1.0 / size))
        block = block - dot_nt(pair[0], off.astype(BF))
        out_ref[:, at:at + size] = block
        yield
        if at + size < width:
            pair = split(block)
            rest = source[:, at + size:]
            shared = split(three(dot_tn, pair, split(rest)))
            yield
            rest_ref[:, at + size:] = rest - three(dot_nn, pair, shared)
            source = rest_ref
            yield


def renew_rows(base_ref, out_ref, work_ref):
    size = base_ref.shape[0]
    group = 64
    work_ref[...] = base_ref[...].T

    def take(turn, carry):
        row = work_ref[pl.ds(turn, 1), :]
        row = row * lax.rsqrt(jnp.sum(row * row, axis=1, keepdims=True))
        work_ref[pl.ds(turn, 1), :] = row

        def clear(which, inner):
            here = pl.ds(pl.multiple_of(which * group, group), group)
            rows = work_ref[here, :]
            later = lax.broadcasted_iota(jnp.int32, (group, 1), 0) + which * group > turn
            share = jnp.where(later, jnp.sum(rows * row, axis=1, keepdims=True), 0.0)
            work_ref[here, :] = rows - share * row
            return inner

        return lax.fori_loop(turn // group, size // group, clear, carry)

    lax.fori_loop(0, size, take, 0)
    out_ref[...] = work_ref[...].T


def move_chain(grad, left_pair, right_pair, weight_ref, first_ref, second_ref, new_ref, copy_ref, first_new_ref, second_new_ref, move_ref):
    rows = grad.shape[0]
    for at in range(0, rows, PIECE):
        size = min(PIECE, rows - at)
        part = slice(at, at + size)
        half = dot_tn(left_pair[0][:, part], grad) + dot_tn(left_pair[1][:, part], grad)
        yield
        turned = three(dot_nn, split(half), right_pair)
        yield
        first_new = BETA_FIRST * first_ref[part, :] + (1.0 - BETA_FIRST) * turned
        second_new = BETA_SECOND * second_ref[part, :] + (1.0 - BETA_SECOND) * turned * turned
        first_new_ref[part, :] = first_new
        second_new_ref[part, :] = second_new
        move_ref[part, :] = (
            first_new
            / (1.0 - BETA_FIRST**STEP)
            / (jnp.sqrt(second_new / (1.0 - BETA_SECOND**STEP)) + EPSILON)
        ).astype(BF)
        yield
    for at in range(0, rows, PIECE):
        part = slice(at, min(at + PIECE, rows))
        back = dot_nn(left_pair[0][part, :], move_ref[...]).astype(BF)
        yield
        new = weight_ref[part, :] * (1.0 - RATE_MATRIX * DECAY_RATE) - RATE_MATRIX * dot_nt(back, right_pair[0])
        new_ref[part, :] = new
        copy_ref[part, :] = new.astype(BF)
        yield


def update_kernel(
    together,
    grad_ref, weight_ref, first_ref, second_ref, left_ref, right_ref,
    grad_out_ref, new_ref, copy_ref, first_new_ref, second_new_ref, left_new_ref, right_new_ref,
    left_base, right_base, left_rest, right_rest, move_ref,
):
    chains = []
    misses = []
    for which in range(together):
        grad = grad_ref[which]
        width = weight_ref.shape[2]
        if grad.shape[1] != width:
            height = weight_ref.shape[1]
            grad = jnp.concatenate([grad[at:at + height] for at in range(0, grad.shape[0], height)], axis=1)
        grad_out_ref[which] = grad.astype(F32)
        left = left_ref[which]
        right = right_ref[which]
        left_pair = split(left)
        right_pair = split(right)
        gram = dot_nt(grad, grad)
        pace = TURN_RATE / (jnp.sqrt(jnp.sum(gram * gram)) + 1e-06)
        left_base[which] = left + dot_nn(gram.astype(BF), left_pair[0]) * pace
        right_base[which] = right + dot_tn(grad, dot_nn(grad, right_pair[0]).astype(BF)) * pace
        misses.append(([], []))
        chains.append(renew_chain(right_base.at[which], right_new_ref.at[which], right_rest.at[which], misses[which][1]))
        chains.append(renew_chain(left_base.at[which], left_new_ref.at[which], left_rest.at[which], misses[which][0]))
        chains.append(
            move_chain(
                grad, left_pair, right_pair, weight_ref.at[which], first_ref.at[which], second_ref.at[which],
                new_ref.at[which], copy_ref.at[which], first_new_ref.at[which], second_new_ref.at[which],
                move_ref.at[which],
            )
        )
    in_step(chains)
    for which in range(together):
        for missed, base, out, rest in zip(
            misses[which], (left_base, right_base), (left_new_ref, right_new_ref), (left_rest, right_rest)
        ):
            worst = functools.reduce(jnp.maximum, missed)

            @pl.when(jnp.logical_not(worst < NEAR))
            def _(base=base, out=out, rest=rest):
                renew_rows(base.at[which], out.at[which], rest.at[which])


def update_stack(grad, skip, together, weight, first, second, left, right):
    slots, rows, width = weight.shape

    def spec(shape):
        return pl.BlockSpec((together,) + shape, lambda slot: (slot, 0, 0))

    flat = spec((rows, width))
    return pl.pallas_call(
        functools.partial(update_kernel, together),
        grid=(slots // together,),
        in_specs=[pl.BlockSpec((together,) + grad.shape[1:], lambda slot: (skip // together + slot, 0, 0))]
        + [flat] * 3 + [spec((rows, rows)), spec((width, width))],
        out_specs=[flat] * 5 + [spec((rows, rows)), spec((width, width))],
        out_shape=[
            jax.ShapeDtypeStruct(weight.shape, F32),
            jax.ShapeDtypeStruct(weight.shape, F32),
            jax.ShapeDtypeStruct(weight.shape, BF),
            jax.ShapeDtypeStruct(weight.shape, F32),
            jax.ShapeDtypeStruct(weight.shape, F32),
            jax.ShapeDtypeStruct(left.shape, F32),
            jax.ShapeDtypeStruct(right.shape, F32),
        ],
        scratch_shapes=[
            pltpu.VMEM((together, rows, rows), F32),
            pltpu.VMEM((together, width, width), F32),
            pltpu.VMEM((together, rows, rows), F32),
            pltpu.VMEM((together, width, width), F32),
            pltpu.VMEM((together, rows, width), BF),
        ],
        compiler_params=pltpu.CompilerParams(vmem_limit_bytes=60 * 1024 * 1024),
        name="rotated_update_%d" % width,
    )(grad, weight, first, second, left, right)


P_SIZE = 197
NBR = 8
HEAD = 64
ROWS = 208
FAR = 200
CHUNK = 256


def layer_norm(values, gain, shift):
    centre = values - jnp.mean(values, axis=-1, keepdims=True)
    scale = lax.rsqrt(jnp.mean(centre * centre, axis=-1, keepdims=True) + 1e-06)
    normal = centre * scale
    return (normal * gain + shift, normal, scale)


def norm_back(grad, normal, scale, gain):
    shaped = grad * gain
    return scale * (
        shaped
        - jnp.mean(shaped, axis=-1, keepdims=True)
        - normal * jnp.mean(shaped * normal, axis=-1, keepdims=True)
    )


def gelu_pair(value):
    size = jnp.abs(value) * (1.0 / math.sqrt(2.0))
    bell = jnp.exp(-0.5 * value * value)
    part = 1.0 / (1.0 + 0.3275911 * size)
    series = part * (
        0.254829592
        + part * (-0.284496736 + part * (1.421413741 + part * (-1.453152027 + part * 1.061405429)))
    )
    tail = 0.5 * series * bell
    share = jnp.where(value < 0.0, tail, 1.0 - tail)
    return value * share, share + value * bell * (1.0 / math.sqrt(2.0 * math.pi))


def block_kernel(
    images,
    core_ref, valid_ref,
    tokens_ref, cotangent_ref, near_ref, norms_ref, attn_ref, mlp_ref,
    out_ref, input_grad_ref, attn_grad_ref, mlp_grad_ref, norm_grad_ref,
    wide, far_f, tokens_f, normed, normal_one, scale_one, query, key, value, probs, mixed,
    middle, normal_two, scale_two, normed_two, cot_low, made, grad_two,
    grad_mid_low, grad_query, grad_key, grad_value,
):
    core = core_ref[0]
    total = tokens_ref.shape[0]
    width = tokens_ref.shape[1]

    def at_own_rows(act):
        for which in range(total // (images * P_SIZE)):

            @pl.when(core == which)
            def _(which=which):
                for image in range(images):
                    act((which * images + image) * P_SIZE, image * ROWS)

    def spread(source, target):
        def act(start, place):
            target[place:place + ROWS, :] = source[start:start + ROWS, :]

        at_own_rows(act)

    pairs = width // (2 * HEAD)
    wide[:total, :] = tokens_ref[...].astype(jnp.float32)
    wide[total:, :] = jnp.zeros((wide.shape[0] - total, width), jnp.float32)
    spread(wide, tokens_f)
    wide[:total, :] = cotangent_ref[...].astype(jnp.float32)
    spread(wide, made)
    far_f[...] = near_ref[...].astype(jnp.float32)
    own_row = lax.broadcasted_iota(jnp.int32, (ROWS, 1), 0) < P_SIZE
    lane = lax.broadcasted_iota(jnp.int32, (1, 2 * HEAD), 1)
    first_head = lane < HEAD
    key_lane = lax.broadcasted_iota(jnp.int32, (1, ROWS), 1)

    def halves(pair):
        zero = jnp.zeros_like(pair)
        return jnp.where(first_head, pair, zero), jnp.where(first_head, zero, pair)

    def step_forward(image, carry):
        here = pl.ds(pl.multiple_of(image * ROWS, ROWS), ROWS)
        x = tokens_f[here, :]
        cot_low[here, :] = jnp.where(own_row, made[here, :], 0.0).astype(BF)
        normed_f, normal, scale = layer_norm(x, norms_ref[0:1, :], norms_ref[1:2, :])
        normal_one[here, :] = normal
        scale_one[here, :] = scale
        allowed = key_lane < P_SIZE
        for slot in range(NBR):
            okay = valid_ref[core * images + image, slot] > 0
            allowed = jnp.logical_or(allowed, jnp.logical_and(key_lane == FAR + slot, okay))
        far = far_f[pl.ds(pl.multiple_of(image * NBR, NBR), NBR), :]
        normed_f = jnp.where(own_row, normed_f, 0.0)
        full = jnp.concatenate([normed_f[:FAR, :], far], axis=0).astype(BF)
        normed[here, :] = full
        q = dot_nt(full, attn_ref[0]).astype(BF)
        k = dot_nt(full, attn_ref[1]).astype(BF)
        v = dot_nt(full, attn_ref[2]).astype(BF)
        query[here, :] = q
        key[here, :] = k
        value[here, :] = v
        bias = jnp.where(allowed, 0.0, -1e30)
        parts = []
        for pair in range(pairs):
            cols = slice(pair * 2 * HEAD, (pair + 1) * 2 * HEAD)
            k_pair = k[:, cols]
            sums = 0.0
            for head, (q_one, v_one) in enumerate(zip(halves(q[:, cols]), halves(v[:, cols]))):
                scores = dot_nt(q_one, k_pair) * 0.125 + bias
                top = jnp.max(scores, axis=-1, keepdims=True)
                powers = jnp.exp(scores - top)
                prob = powers / jnp.sum(powers, axis=-1, keepdims=True)
                probs[image * 2 * pairs + 2 * pair + head] = prob
                sums = sums + dot_nn(prob.astype(BF), v_one)
            parts.append(sums.astype(BF))
        mix = jnp.concatenate(parts, axis=1)
        mixed[here, :] = mix
        mid = x + dot_nn(mix, attn_ref[3])
        middle[here, :] = mid
        two_f, normal, scale = layer_norm(mid, norms_ref[2:3, :], norms_ref[3:4, :])
        normal_two[here, :] = normal
        scale_two[here, :] = scale
        normed_two[here, :] = two_f.astype(BF)
        return carry

    lax.fori_loop(0, images, step_forward, 0)

    made[...] = jnp.zeros_like(made)
    grad_two[...] = jnp.zeros_like(grad_two)
    chunks = mlp_ref.shape[3] // CHUNK

    def step_mlp(turn, carry):
        half = turn // chunks
        cols = pl.ds(pl.multiple_of((turn % chunks) * CHUNK, CHUNK), CHUNK)
        w_one = mlp_ref[0, half, :, cols]
        w_two = mlp_ref[1, half, :, cols]
        two = normed_two[...]
        cot = cot_low[...]
        hidden, slope = gelu_pair(dot_nn(two, w_one))
        hidden = hidden.astype(BF)
        grad_inner = (dot_nn(cot, w_two) * slope).astype(BF)
        made[...] += dot_nt(hidden, w_two)
        grad_two[...] += dot_nt(grad_inner, w_one)
        mlp_grad_ref[0, half, :, cols] = dot_tn(two, grad_inner)
        mlp_grad_ref[1, half, :, cols] = dot_tn(cot, hidden)
        return carry

    lax.fori_loop(0, 2 * chunks, step_mlp, 0)

    norm_grad_ref[...] = jnp.zeros_like(norm_grad_ref)
    input_grad_ref[...] = jnp.zeros_like(input_grad_ref)
    wide[...] = jnp.zeros_like(wide)

    def step_backward(image, carry):
        here = pl.ds(pl.multiple_of(image * ROWS, ROWS), ROWS)
        made[here, :] += middle[here, :]
        grad_n = grad_two[here, :]
        normal = normal_two[here, :]
        norm_grad_ref[2:3, :] += jnp.sum(grad_n * normal, axis=0, keepdims=True)
        norm_grad_ref[3:4, :] += jnp.sum(grad_n, axis=0, keepdims=True)
        grad_mid = cot_low[here, :].astype(jnp.float32) + norm_back(
            grad_n, normal, scale_two[here, :], norms_ref[2:3, :]
        )
        low = grad_mid.astype(BF)
        grad_mid_low[here, :] = low
        grad_mix = dot_nt(low, attn_ref[3]).astype(BF)
        q = query[here, :]
        k = key[here, :]
        v = value[here, :]
        parts_q, parts_k, parts_v = [], [], []
        for pair in range(pairs):
            cols = slice(pair * 2 * HEAD, (pair + 1) * 2 * HEAD)
            gm_pair = grad_mix[:, cols]
            sum_q = sum_k = sum_v = 0.0
            for head, (q_one, k_one, v_one, gm_one) in enumerate(
                zip(halves(q[:, cols]), halves(k[:, cols]), halves(v[:, cols]), halves(gm_pair))
            ):
                prob = probs[image * 2 * pairs + 2 * pair + head]
                grad_prob = dot_nt(gm_pair, v_one)
                sum_v = sum_v + dot_tn(prob.astype(BF), gm_one)
                weighed = prob * grad_prob
                grad_score = (
                    weighed - prob * jnp.sum(weighed, axis=-1, keepdims=True)
                ).astype(BF)
                sum_q = sum_q + dot_nn(grad_score, k_one)
                sum_k = sum_k + dot_tn(grad_score, q_one)
            parts_q.append((sum_q * 0.125).astype(BF))
            parts_k.append((sum_k * 0.125).astype(BF))
            parts_v.append(sum_v.astype(BF))
        gq = jnp.concatenate(parts_q, axis=1)
        gk = jnp.concatenate(parts_k, axis=1)
        gv = jnp.concatenate(parts_v, axis=1)
        grad_query[here, :] = gq
        grad_key[here, :] = gk
        grad_value[here, :] = gv
        grad_n = dot_nn(gq, attn_ref[0]) + dot_nn(gk, attn_ref[1]) + dot_nn(gv, attn_ref[2])
        grad_n = jnp.where(own_row, grad_n, 0.0)
        normal = normal_one[here, :]
        norm_grad_ref[0:1, :] += jnp.sum(grad_n * normal, axis=0, keepdims=True)
        norm_grad_ref[1:2, :] += jnp.sum(grad_n, axis=0, keepdims=True)
        back = grad_mid + norm_back(grad_n, normal, scale_one[here, :], norms_ref[0:1, :])
        middle[here, :] = back
        return carry

    lax.fori_loop(0, images, step_backward, 0)

    def pack(start, place):
        wide[start:start + P_SIZE, :] = made[place:place + P_SIZE, :]
        input_grad_ref[start:start + P_SIZE, :] = middle[place:place + P_SIZE, :]

    at_own_rows(pack)
    out_ref[...] = wide[:total, :].astype(BF)
    attn_grad_ref[0] = dot_tn(grad_query[...], normed[...])
    attn_grad_ref[1] = dot_tn(grad_key[...], normed[...])
    attn_grad_ref[2] = dot_tn(grad_value[...], normed[...])
    attn_grad_ref[3] = dot_tn(mixed[...], grad_mid_low[...])


def block(core, nbr_valid, tokens, cotangent, near, norms, attn, mlp):
    total, width = tokens.shape
    images = nbr_valid.shape[0] // mlp.shape[1]
    rows = images * ROWS
    padded = total + 16 - total % 8
    f32 = jnp.float32
    vmem = pl.BlockSpec(memory_space=pltpu.VMEM)
    smem = pl.BlockSpec(memory_space=pltpu.SMEM)
    heads = width // HEAD
    flat_f = pltpu.VMEM((rows, width), f32)
    flat_low = pltpu.VMEM((rows, width), BF)
    column = pltpu.VMEM((rows, 1), f32)
    return pl.pallas_call(
        functools.partial(block_kernel, images),
        in_specs=[smem] * 2 + [vmem] * 6,
        out_specs=[vmem] * 5,
        out_shape=[
            jax.ShapeDtypeStruct((total, width), BF),
            jax.ShapeDtypeStruct((total, width), f32),
            jax.ShapeDtypeStruct(attn.shape, f32),
            jax.ShapeDtypeStruct(mlp.shape, f32),
            jax.ShapeDtypeStruct((4, width), f32),
        ],
        scratch_shapes=[
            pltpu.VMEM((padded, width), f32),
            pltpu.VMEM(near.shape, f32),
            flat_f,
            flat_low, flat_f, column, flat_low, flat_low, flat_low,
            pltpu.VMEM((images * heads, ROWS, ROWS), f32),
            flat_low,
            flat_f, flat_f, column, flat_low, flat_low, flat_f, flat_f,
            flat_low, flat_low, flat_low, flat_low,
        ],
        compiler_params=pltpu.CompilerParams(vmem_limit_bytes=60 * 1024 * 1024),
        name="block_both_ways",
    )(core, nbr_valid, tokens, cotangent, near, norms, attn, mlp)


MESH = pl.DeviceIdType.MESH


def fetch_kernel(
    chips, picks,
    wanted_ref, queue_ref, attn_ref, mlp_ref,
    near_ref, attn_out, mlp_out,
    asked, given, parts, ask_send, ask_recv, give_send, give_recv, swap_send, swap_recv,
):
    me = lax.axis_index("dp")
    core = lax.axis_index("mp")
    other = 1 - core
    depth = queue_ref.shape[0]
    barrier = pltpu.get_barrier_semaphore()
    pl.semaphore_signal(barrier, inc=1, device_id=(me, other), device_id_type=MESH)

    def greet(hop, carry):
        pl.semaphore_signal(
            barrier, inc=1, device_id=(lax.rem(me + hop, chips), core), device_id_type=MESH
        )
        return carry

    lax.fori_loop(1, chips, greet, 0)
    attn_out[:, core] = attn_ref[...].astype(BF)
    mlp_out[:, core] = mlp_ref[...].astype(BF)
    pl.semaphore_wait(barrier, chips)

    def ask(hop):
        return pltpu.make_async_remote_copy(
            src_ref=wanted_ref.at[core],
            dst_ref=asked.at[hop],
            send_sem=ask_send.at[hop],
            recv_sem=ask_recv.at[hop],
            device_id=(lax.rem(me + hop, chips), core),
            device_id_type=MESH,
        )

    def give(hop):
        return pltpu.make_async_remote_copy(
            src_ref=parts.at[hop],
            dst_ref=given.at[hop],
            send_sem=give_send.at[hop],
            recv_sem=give_recv.at[hop],
            device_id=(lax.rem(me + chips - hop, chips), core),
            device_id_type=MESH,
        )

    def start_ask(hop, carry):
        ask(hop).start()
        return carry

    lax.fori_loop(1, chips, start_ask, 0)
    swaps = [
        pltpu.make_async_remote_copy(
            src_ref=out.at[:, core],
            dst_ref=out.at[:, core],
            send_sem=swap_send.at[place],
            recv_sem=swap_recv.at[place],
            device_id=(me, other),
            device_id_type=MESH,
        )
        for place, out in enumerate((attn_out, mlp_out))
    ]
    for swap in swaps:
        swap.start()
    places = lax.broadcasted_iota(jnp.int32, (picks, depth), 1) + me * depth

    def choose(wanted):
        chooser = jnp.where(wanted == places, 1.0, 0.0).astype(BF)
        return dot_nn(chooser, queue_ref[...]).astype(BF)

    given[0] = choose(wanted_ref[core])

    def answer(hop, carry):
        ask(hop).wait_recv()
        parts[hop] = choose(asked[hop])
        give(hop).start()
        return carry

    lax.fori_loop(1, chips, answer, 0)

    def collect(hop, total):
        give(hop).wait_recv()
        return total + given[hop].astype(jnp.float32)

    total = lax.fori_loop(1, chips, collect, given[0].astype(jnp.float32))
    near_ref[...] = total.astype(BF)

    def finish(hop, carry):
        ask(hop).wait_send()
        give(hop).wait_send()
        return carry

    lax.fori_loop(1, chips, finish, 0)
    for swap in swaps:
        swap.wait()


def fetch(chips, wanted, queue, attn, mlp):
    cores, picks, lanes = wanted.shape
    vmem = pl.BlockSpec(memory_space=pltpu.VMEM)
    width = queue.shape[1]
    return pl.pallas_call(
        functools.partial(fetch_kernel, chips, picks),
        in_specs=[vmem] * 4,
        out_specs=[vmem] * 3,
        out_shape=[
            jax.ShapeDtypeStruct((picks, width), BF),
            jax.ShapeDtypeStruct((attn.shape[0], cores) + attn.shape[1:], BF),
            jax.ShapeDtypeStruct((mlp.shape[0], cores) + mlp.shape[1:], BF),
        ],
        scratch_shapes=[
            pltpu.VMEM((chips, picks, lanes), jnp.int32),
            pltpu.VMEM((chips, picks, width), BF),
            pltpu.VMEM((chips, picks, width), BF),
            pltpu.SemaphoreType.DMA((chips,)),
            pltpu.SemaphoreType.DMA((chips,)),
            pltpu.SemaphoreType.DMA((chips,)),
            pltpu.SemaphoreType.DMA((chips,)),
            pltpu.SemaphoreType.DMA((2,)),
            pltpu.SemaphoreType.DMA((2,)),
        ],
        compiler_params=pltpu.CompilerParams(
            collective_id=0, has_side_effects=True, vmem_limit_bytes=48 * 1024 * 1024
        ),
        name="fetch",
    )(wanted, queue, attn, mlp)


HALVINGS = 4


def orders(bits):
    base = list(range(bits))
    if bits < 3:
        return [base, base[::-1], base]
    low = base[:2]
    return [base, low[::-1] + base[2:], base[2:4] + low + base[4:]]


def sum_kernel(
    bits,
    attn_ref, mlp_ref, norm_ref,
    done, norm_out,
    total, first_send, first_recv, sent, recv, norm_recv, norm_work,
    swap_send, swap_recv, step_send, step_recv, spread_send, spread_recv, norm_send, norm_sem,
):
    me = lax.axis_index("dp")
    core = lax.axis_index("mp")
    other = 1 - core
    slots, cores, rows, width = attn_ref.shape
    height = slots * rows
    halvings = min(HALVINGS, bits)
    plan = orders(bits)
    parts = 3

    def mate(bit):
        return me + (1 - 2 * ((me // 2**bit) % 2)) * 2**bit

    barrier = pltpu.get_barrier_semaphore()
    pl.semaphore_signal(barrier, inc=1, device_id=(me, other), device_id_type=MESH)
    for bit in range(bits):
        pl.semaphore_signal(barrier, inc=1, device_id=(mate(bit), core), device_id_type=MESH)

    def fill(target, part, whose, cast):
        if part < 2:
            for block in range(mlp_ref.shape[3] // width):
                target[part, block * mlp_ref.shape[2]:(block + 1) * mlp_ref.shape[2], :] = mlp_ref[
                    part, whose, :, block * width:(block + 1) * width
                ].astype(cast)
        else:
            for slot in range(slots):
                target[part, slot * rows:(slot + 1) * rows, :] = attn_ref[slot, whose].astype(cast)

    for part in range(parts):
        fill(first_send, part, other, BF)
    pl.semaphore_wait(barrier, bits + 1)

    def copy(src, dst, send, recv, device):
        return pltpu.make_async_remote_copy(
            src_ref=src, dst_ref=dst, send_sem=send, recv_sem=recv, device_id=device, device_id_type=MESH
        )

    pending = []
    swaps = []
    for part in range(parts):
        swap = copy(first_send.at[part], first_recv.at[part], swap_send.at[part], swap_recv.at[part], (me, other))
        swap.start()
        swaps.append(swap)
    norm_work[0] = norm_ref[...]
    norm_copy = copy(norm_work.at[0], norm_recv.at[0], norm_send.at[0], norm_sem.at[0], (me, other))
    norm_copy.start()
    for part in range(parts):
        fill(total, part, core, jnp.float32)

    offsets = [0] * parts
    size = height
    copies = [None] * parts
    for step in range(halvings + 1):
        half = size // 2
        for part in range(parts):
            held = pl.ds(pl.multiple_of(offsets[part], 16), size)
            if step == 0:
                swaps[part].wait_recv()
                arrived = first_recv.at[part]
            else:
                copies[part].wait_recv()
                arrived = recv.at[part, pl.ds(height - 2 * size, size)]
            total[part, held, :] += arrived[...].astype(jnp.float32)
            if step < halvings:
                bit = plan[part][step]
                mine = (me // 2**bit) % 2
                away = pl.multiple_of(offsets[part] + (1 - mine) * half, 16)
                slot = pl.ds(height - 2 * half, half)
                sent[part, slot, :] = total[part, pl.ds(away, half), :].astype(BF)
                copies[part] = copy(
                    sent.at[part, slot],
                    recv.at[part, slot],
                    step_send.at[part, step],
                    step_recv.at[part, step],
                    (mate(bit), core),
                )
                copies[part].start()
                pending.append(copies[part])
                offsets[part] = offsets[part] + mine * half
        if step < halvings:
            size = half
    for step in range(bits + 1):
        norm_copy.wait()
        if step < bits:
            norm_work[step + 1] = norm_work[step] + norm_recv[step]
            norm_copy = copy(
                norm_work.at[step + 1],
                norm_recv.at[step + 1],
                norm_send.at[step + 1],
                norm_sem.at[step + 1],
                (mate(step), core),
            )
            norm_copy.start()
        else:
            norm_out[...] = norm_work[step] + norm_recv[step]
    for step in range(halvings, bits):
        for part in range(parts):
            bit = plan[part][step]
            held = pl.ds(pl.multiple_of(offsets[part], 16), size)
            place = height + (step - halvings) * size
            slot = pl.ds(place, size)
            sent[part, slot, :] = total[part, held, :].astype(BF)
            copies[part] = copy(
                sent.at[part, slot],
                recv.at[part, slot],
                step_send.at[part, step],
                step_recv.at[part, step],
                (mate(bit), core),
            )
            copies[part].start()
            pending.append(copies[part])
        for part in range(parts):
            held = pl.ds(pl.multiple_of(offsets[part], 16), size)
            slot = pl.ds(height + (step - halvings) * size, size)
            copies[part].wait_recv()
            total[part, held, :] = sent[part, slot, :].astype(jnp.float32) + recv[part, slot, :].astype(jnp.float32)
    for part in range(parts):
        held = pl.ds(pl.multiple_of(offsets[part], 16), size)
        done[part, held, :] = total[part, held, :].astype(BF)
    for back in range(halvings):
        step = halvings - 1 - back
        for part in range(parts):
            bit = plan[part][step]
            held = pl.ds(pl.multiple_of(offsets[part], 16), size)
            copies[part] = copy(
                done.at[part, held],
                done.at[part, held],
                spread_send.at[part, step],
                spread_recv.at[part, step],
                (mate(bit), core),
            )
            if back > 0:
                previous[part].wait_recv()
            copies[part].start()
            pending.append(copies[part])
            mine = (me // 2**bit) % 2
            offsets[part] = offsets[part] - mine * size
        previous = list(copies)
        size = size * 2
    for part in range(parts):
        previous[part].wait_recv()
    for one in swaps + pending:
        one.wait_send()


def sum_grads(chips, attn, mlp, norm):
    bits = chips.bit_length() - 1
    slots, cores, rows, width = attn.shape
    height = slots * rows
    halvings = min(HALVINGS, bits)
    tall = height + (bits - halvings) * (height >> halvings)
    vmem = pl.BlockSpec(memory_space=pltpu.VMEM)
    f32 = jnp.float32
    dma = pltpu.SemaphoreType.DMA
    return pl.pallas_call(
        functools.partial(sum_kernel, bits),
        in_specs=[vmem] * 3,
        out_specs=[vmem] * 2,
        out_shape=[
            jax.ShapeDtypeStruct((3, height, width), BF),
            jax.ShapeDtypeStruct(norm.shape, f32),
        ],
        scratch_shapes=[
            pltpu.VMEM((3, height, width), f32),
            pltpu.VMEM((3, height, width), BF),
            pltpu.VMEM((3, height, width), BF),
            pltpu.VMEM((3, tall, width), BF),
            pltpu.VMEM((3, tall, width), BF),
            pltpu.VMEM((bits + 1,) + norm.shape, f32),
            pltpu.VMEM((bits + 1,) + norm.shape, f32),
            dma((3,)), dma((3,)),
            dma((3, bits)), dma((3, bits)),
            dma((3, halvings)), dma((3, halvings)),
            dma((bits + 1,)), dma((bits + 1,)),
        ],
        compiler_params=pltpu.CompilerParams(
            collective_id=1, has_side_effects=True, vmem_limit_bytes=60 * 1024 * 1024
        ),
        name="sum_grads",
    )(attn, mlp, norm)


RATE_NORM = 0.6


def body(
    chips,
    tokens,
    cotangent,
    queue,
    nbr_index,
    nbr_valid,
    norm_params,
    norm_first,
    norm_second,
    attn_weight,
    mlp_weight,
    attn_first,
    attn_second,
    mlp_first,
    mlp_second,
    attn_left,
    attn_right,
    mlp_left,
    mlp_right,
):
    def flip(value):
        return value.transpose(0, 2, 1)

    core = lax.axis_index("mp").reshape(1)
    cores = attn_weight.shape[1] // attn_weight.shape[2]
    picks = nbr_index.size // cores
    wanted = jnp.broadcast_to(nbr_index.reshape(cores, picks, 1), (cores, picks, queue.shape[0]))
    attn_own = flip(attn_weight)
    near, attn_low, mlp_low = fetch(chips, wanted, queue, attn_own, mlp_weight)
    width = queue.shape[1]
    block_out, input_grad, attn_part, mlp_part, norm_part = block(
        core,
        nbr_valid,
        tokens,
        cotangent,
        near,
        norm_params,
        attn_low.reshape(attn_low.shape[0], width, width),
        mlp_low,
    )
    summed, norm_grad = sum_grads(chips, attn_part.reshape(attn_low.shape), mlp_part, norm_part)
    block_out = lax.psum(block_out, "mp")
    input_grad = lax.psum(input_grad, "mp")
    norm_first_new = BETA_FIRST * norm_first + (1.0 - BETA_FIRST) * norm_grad
    norm_second_new = BETA_SECOND * norm_second + (1.0 - BETA_SECOND) * norm_grad * norm_grad
    norm_new = norm_params - RATE_NORM * (norm_first_new / (1.0 - BETA_FIRST**STEP)) / (
        jnp.sqrt(norm_second_new / (1.0 - BETA_SECOND**STEP)) + EPSILON
    )
    slots, rows, width = attn_own.shape
    (
        mlp_grad,
        mlp_new,
        mlp_copy,
        mlp_first_new,
        mlp_second_new,
        mlp_left_new,
        mlp_right_new,
    ) = update_stack(
        summed, 0, 1, mlp_weight, mlp_first, mlp_second, mlp_left, mlp_right
    )
    (
        attn_grad,
        attn_new,
        attn_copy,
        attn_first_new,
        attn_second_new,
        attn_right_new,
        attn_left_new,
    ) = update_stack(
        summed.reshape(-1, rows, width),
        2 * slots,
        2,
        attn_own,
        flip(attn_first),
        flip(attn_second),
        attn_right,
        attn_left,
    )
    return (
        block_out,
        input_grad,
        norm_grad,
        flip(attn_grad),
        mlp_grad,
        norm_first_new,
        norm_second_new,
        norm_new,
        flip(attn_first_new),
        flip(attn_second_new),
        mlp_first_new,
        mlp_second_new,
        attn_left_new,
        attn_right_new,
        mlp_left_new,
        mlp_right_new,
        flip(attn_new),
        flip(attn_copy),
        mlp_new,
        mlp_copy,
    )


def solution(mesh):
    return jax.shard_map(
        functools.partial(body, mesh.shape["dp"]),
        mesh=mesh,
        in_specs=(
            P("dp", None),
            P("dp", None),
            P("dp", None),
            P("dp", None),
            P("dp", None),
            P(),
            P(),
            P(),
            P(None, None, "mp"),
            P(None, None, "mp"),
            P(None, None, "mp"),
            P(None, None, "mp"),
            P(None, None, "mp"),
            P(None, None, "mp"),
            P(None, "mp", None),
            P(None, "mp", None),
            P(None, "mp", None),
            P(None, "mp", None),
        ),
        out_specs=(
            P("dp", None),
            P("dp", None),
            P(),
            P(None, None, "mp"),
            P(None, None, "mp"),
            P(),
            P(),
            P(),
            P(None, None, "mp"),
            P(None, None, "mp"),
            P(None, None, "mp"),
            P(None, None, "mp"),
            P(None, "mp", None),
            P(None, "mp", None),
            P(None, "mp", None),
            P(None, "mp", None),
            P(None, None, "mp"),
            P(None, None, "mp"),
            P(None, None, "mp"),
            P(None, None, "mp"),
        ),
        check_vma=False,
    )
```

profile of v0, /device:TPU:0, one launch (start us, length us, event | category | flops | bytes accessed | tf_op | source)
XLA Modules:
  0.0 217.6 jit_solution(10610019786966574513)
XLA Ops:
  7.2 0.0 all-reduce.3.cloned.1.call-start
  7.2 0.8 broadcast_in_dim.7
  8.0 0.1 broadcast_in_dim.8.wanted_ref
  8.1 0.0 copy-start
  8.1 1.3 copy-done
  9.4 0.0 copy-start.3
  9.4 0.9 copy-done.3
  10.2 27.8 %fetch.1 = (bf16[32,384]{1,0:T(8,128)(2,1)S(1)}, bf16[4,2,192,384]{3,2,1,0:T(8,128)(2,1)S(1)}, bf16[2,2,384,768]{3,2,1,0:T(8,128)(2,1)S(1)}) custom-call(s32[2,32,128]{2,1,0:T(8,128)S(1)} %broadcast_in_dim.8.wanted_ref, bf16[128,384]{1,0:T(8,128)(2,1)S(1)} %copy-done.3, f32[4,192,384]{2,1,0:T(8,128)S(1)} %bitcast.13, f32[2,384,768]{2,1,0:T(8,128)} %weight_ref.1), custom_call_target="tpu_custom_call" | custom-call | tf_op jit(solution)/shard_map/fetch/pallas_call | solution.py:607
  38.1 0.0 copy-start.1
  38.1 1.4 copy-done.1
  39.5 1.0 copy-done.2
  40.5 0.6 copy-done.4
  41.1 37.5 %block_both_ways.1 = (bf16[1576,384]{1,0:T(8,128)(2,1)}, f32[1576,384]{1,0:T(8,128)}, f32[4,384,384]{2,1,0:T(8,128)}, f32[2,2,384,768]{3,2,1,0:T(8,128)}, f32[4,384]{1,0:T(4,128)}) custom-call(s32[1]{0:T(128)} %bitcast.core_ref, s32[8,8]{1,0:T(8,128)} %valid_ref.1, bf16[1576,384]{1,0:T(8,128)(2,1)} %tokens_ref.1, bf16[1576,384]{1,0:T(8,128)(2,1)} %cotangent_ref.1, ...), custom_call_target="tpu_custom_call" | custom-call | tf_op jit(solution)/shard_map/block_both_ways/pallas_call | solution.py:479
  78.6 0.0 all-reduce.3.cloned.1.call-update
  78.7 0.0 all-reduce.5.cloned.1.call-start
  78.7 0.7 all-reduce.5.cloned.1.call-update
  79.4 63.7 %sum_grads.1 = (bf16[3,768,384]{2,1,0:T(8,128)(2,1)}, f32[4,384]{1,0:T(4,128)}) custom-call(f32[4,2,192,384]{3,2,1,0:T(8,128)} %bitcast.16, f32[2,2,384,768]{3,2,1,0:T(8,128)} %get-tuple-element.50.mlp_ref, f32[4,384]{1,0:T(4,128)} %get-tuple-element.51.norm_ref), custom_call_target="tpu_custom_call" | custom-call | tf_op jit(solution)/shard_map/sum_grads/pallas_call | solution.py:805
  143.1 39.8 %rotated_update_768.1 = (f32[2,384,768]{2,1,0:T(8,128)}, f32[2,384,768]{2,1,0:T(8,128)}, bf16[2,384,768]{2,1,0:T(8,128)(2,1)}, f32[2,384,768]{2,1,0:T(8,128)}, f...) custom-call(bf16[3,768,384]{2,1,0:T(8,128)(2,1)} %get-tuple-element.53.grad_ref, ...), custom_call_target="tpu_custom_call" | custom-call | tf_op jit(solution)/shard_map/rotated_update_768/pallas_call | solution.py:222
  183.0 0.0 copy-start.6
  183.0 0.0 copy-start.7
  183.0 0.0 copy-start.8
  183.0 0.0 copy-start.9
  183.0 22.4 %rotated_update_384.1 = (f32[4,192,384]{2,1,0:T(8,128)}, f32[4,192,384]{2,1,0:T(8,128)}, bf16[4,192,384]{2,1,0:T(8,128)(2,1)}, f32[4,192,384]{2,1,0:T(8,128)}, f...) custom-call(bf16[12,192,384]{2,1,0:T(8,128)(2,1)} %bitcast.15, f32[4,192,384]{2,1,0:T(8,128)} %bitcast.12, ...), custom_call_target="tpu_custom_call" | custom-call | tf_op jit(solution)/shard_map/rotated_update_384/pallas_call | solution.py:222
  205.5 0.0 copy-done.6
  205.5 0.0 copy-done.7
  205.5 0.0 copy-done.8
  205.5 0.0 copy-done.9
  205.5 0.6 divide_subtract_fusion
  206.1 2.6 %copy.41 = bf16[1576,384]{1,0:T(8,128)(2,1)} copy(bf16[1576,384]{1,0:T(8,128)(2,1)} %all-reduce.3.cloned.1.call-done) | data formatting | bytes 2420736
  208.7 0.0 copy-done.5
  208.7 1.4 copy.42
  210.1 0.6 copy.43
  (5 shorter events, 0.0 us)
Async XLA Ops:
  7.2 198.9 %all-reduce.3.cloned.1.call-start = ((), (), s32[]{:S(2)}) async-start(), calls=%async_computation | async-start | bytes 2420736 | tf_op jit(solution)/shard_map/psum | solution.py:878
  8.1 1.3 copy-start
  9.4 0.9 copy-start.3
  38.1 1.4 copy-start.1
  39.5 1.0 copy-start.2
  40.5 0.6 copy-start.4
  78.7 127.5 %all-reduce.5.cloned.1.call-start = ((), (), s32[]{:S(2)}) async-start(), calls=%async_computation.1 | async-start | bytes 4841472 | tf_op jit(solution)/shard_map/psum | solution.py:879
  183.0 22.5 %copy-start.6 = (f32[4,384]{1,0:T(4,128)S(1)}, f32[4,384]{1,0:T(4,128)}, u32[]{:S(2)}) copy-start(f32[4,384]{1,0:T(4,128)} %norms_ref.1) | copy-start | bytes 18436
  183.0 22.5 %copy-start.7 = (f32[4,384]{1,0:T(4,128)S(1)}, f32[4,384]{1,0:T(4,128)}, u32[]{:S(2)}) copy-start(f32[4,384]{1,0:T(4,128)} %get-tuple-element.93) | copy-start | bytes 18436
  183.0 22.5 %copy-start.8 = (f32[4,384]{1,0:T(4,128)S(1)}, f32[4,384]{1,0:T(4,128)}, u32[]{:S(2)}) copy-start(f32[4,384]{1,0:T(4,128)} %param.25) | copy-start | bytes 18436
  183.0 22.5 %copy-start.9 = (f32[4,384]{1,0:T(4,128)S(1)}, f32[4,384]{1,0:T(4,128)}, u32[]{:S(2)}) copy-start(f32[4,384]{1,0:T(4,128)} %param.24) | copy-start | bytes 18436
  206.1 2.6 %copy-start.5 = (f32[1576,384]{1,0:T(8,128)S(1)}, f32[1576,384]{1,0:T(8,128)}, u32[]{:S(2)}) copy-start(f32[1576,384]{1,0:T(8,128)} %all-reduce.5.cloned.1.call-done) | copy-start | bytes 7262212
Sparse Core Ops, SparseCore 0:
  78.8 15.9 all-reduce.2
  97.7 22.8 all-reduce.4
where the time goes:
time: 218 us
  Pallas kernels  191 us (88%)
  between operations  14.2 us (7%)
  local copies, waits for them, and re-layouts  10.6 us (5%)
    pallas_call x1, Pallas kernels, sum_grads(): pl.pallas_call(functools.partial(sum_kernel, bits), in_specs=[vmem] * 3,...  63.7 us
    pallas_call x2, Pallas kernels, update_stack(): pl.pallas_call(functools.partial(update_kernel, together), grid=(slots //...  62.3 us
    pallas_call x1, Pallas kernels, block(): pl.pallas_call(functools.partial(block_kernel, images), in_specs=[smem] *...  37.5 us
    pallas_call x1, Pallas kernels, fetch(): pl.pallas_call(functools.partial(fetch_kernel, chips, picks), in_specs=[v...  27.8 us
    unnamed x23, local copies, waits for them, and re-layouts  9.81 us
  transfers between devices with their start and end apart: 2, of which 0 were waited for; matrix products, arithmetic and copies ran while one was open for 0% of the time, Pallas kernels for 58%

commit v1 on v0

v1 whole, which is shorter than its diff:
```python
import functools
import math

import jax
import jax.numpy as jnp
from jax import lax
from jax.experimental import pallas as pl
from jax.experimental.pallas import tpu as pltpu
from jax.sharding import PartitionSpec as P

BETA_FIRST = 0.9
BETA_SECOND = 0.95
EPSILON = 1e-08
RATE_MATRIX = 0.15
DECAY_RATE = 0.05
TURN_RATE = 4.0
STEP = 10
BLOCK = 256
ROUNDS = 3
NEAR = 0.01
PIECE = 128

BF = jnp.bfloat16
F32 = jnp.float32


def dot_nn(a, b):
    return lax.dot_general(a, b, (((1,), (0,)), ((), ())), preferred_element_type=F32)


def dot_nt(a, b):
    return lax.dot_general(a, b, (((1,), (1,)), ((), ())), preferred_element_type=F32)


def dot_tn(a, b):
    return lax.dot_general(a, b, (((0,), (0,)), ((), ())), preferred_element_type=F32)


def split(a):
    high = a.astype(BF)
    return high, (a - high.astype(F32)).astype(BF)


def three(dot, a, b):
    return dot(a[0], b[0]) + (dot(a[0], b[1]) + dot(a[1], b[0]))


def below(size):
    row = lax.broadcasted_iota(jnp.int32, (size, size), 0)
    col = lax.broadcasted_iota(jnp.int32, (size, size), 1)
    return row > col, row == col


def in_step(chains):
    chains = list(chains)
    while chains:
        kept = []
        for chain in chains:
            try:
                next(chain)
                kept.append(chain)
            except StopIteration:
                pass
        chains = kept


def renew_chain(base_ref, out_ref, rest_ref, misses):
    width = base_ref.shape[1]
    source = base_ref
    for at in range(0, width, BLOCK):
        size = min(BLOCK, width - at)
        lower, same = below(size)
        eye = jnp.where(same, 1.0, 0.0)
        low = source[:, at:at + size].astype(BF)
        gram = dot_tn(low, low)
        yield
        on_diag = jnp.where(same, gram, 0.0)
        s_col = lax.rsqrt(jnp.maximum(jnp.sum(on_diag, axis=1, keepdims=True), 1e-30))
        s_row = lax.rsqrt(jnp.maximum(jnp.sum(on_diag, axis=0, keepdims=True), 1e-30))
        state = gram * s_col * s_row
        made = jnp.where(same, s_col, 0.0).astype(BF)
        for turn in range(ROUNDS):
            under = jnp.where(lower, state, 0.0)
            moved = dot_nn(under.astype(BF), state.astype(BF))
            mass = jnp.sum(under * under, axis=1, keepdims=True)
            yield
            curve = jnp.sum(moved * under, axis=1, keepdims=True)
            pace = jnp.where(curve > mass, mass / jnp.maximum(curve, 1e-30), 1.0)
            left = 1.0 - 2.0 * pace * mass + pace * pace * curve
            scale = lax.rsqrt(jnp.maximum(left, 1e-6))
            step = (scale * (eye - pace * under)).astype(BF)
            if turn + 1 < ROUNDS:
                state = dot_nt((scale * (state - pace * moved)).astype(BF), step)
            made = dot_nn(step, made).astype(BF)
            yield
        high, low = split(source[:, at:at + size])
        block = dot_nt(high, made) + dot_nt(low, made)
        yield
        pair = split(block)
        gram = three(dot_tn, pair, pair)
        yield
        off = jnp.where(lower, gram, 0.0) + jnp.where(same, 0.5 * (gram - 1.0), 0.0)
        misses.append(jnp.sum(off * off) * (1.0 / size))
        block = block - dot_nt(pair[0], off.astype(BF))
        out_ref[:, at:at + size] = block
        yield
        if at + size < width:
            pair = split(block)
            rest = source[:, at + size:]
            shared = split(three(dot_tn, pair, split(rest)))
            yield
            rest_ref[:, at + size:] = rest - three(dot_nn, pair, shared)
            source = rest_ref
            yield


def renew_rows(base_ref, out_ref, work_ref):
    size = base_ref.shape[0]
    group = 64
    work_ref[...] = base_ref[...].T

    def take(turn, carry):
        row = work_ref[pl.ds(turn, 1), :]
        row = row * lax.rsqrt(jnp.sum(row * row, axis=1, keepdims=True))
        work_ref[pl.ds(turn, 1), :] = row

        def clear(which, inner):
            here = pl.ds(pl.multiple_of(which * group, group), group)
            rows = work_ref[here, :]
            later = lax.broadcasted_iota(jnp.int32, (group, 1), 0) + which * group > turn
            share = jnp.where(later, jnp.sum(rows * row, axis=1, keepdims=True), 0.0)
            work_ref[here, :] = rows - share * row
            return inner

        return lax.fori_loop(turn // group, size // group, clear, carry)

    lax.fori_loop(0, size, take, 0)
    out_ref[...] = work_ref[...].T


def move_chain(grad, left_pair, right_pair, weight_ref, first_ref, second_ref, new_ref, copy_ref, first_new_ref, second_new_ref, move_ref):
    rows = grad.shape[0]
    for at in range(0, rows, PIECE):
        size = min(PIECE, rows - at)
        part = slice(at, at + size)
        half = dot_tn(left_pair[0][:, part], grad) + dot_tn(left_pair[1][:, part], grad)
        yield
        turned = three(dot_nn, split(half), right_pair)
        yield
        first_new = BETA_FIRST * first_ref[part, :] + (1.0 - BETA_FIRST) * turned
        second_new = BETA_SECOND * second_ref[part, :] + (1.0 - BETA_SECOND) * turned * turned
        first_new_ref[part, :] = first_new
        second_new_ref[part, :] = second_new
        move_ref[part, :] = (
            first_new
            / (1.0 - BETA_FIRST**STEP)
            / (jnp.sqrt(second_new / (1.0 - BETA_SECOND**STEP)) + EPSILON)
        ).astype(BF)
        yield
    for at in range(0, rows, PIECE):
        part = slice(at, min(at + PIECE, rows))
        back = dot_nn(left_pair[0][part, :], move_ref[...]).astype(BF)
        yield
        new = weight_ref[part, :] * (1.0 - RATE_MATRIX * DECAY_RATE) - RATE_MATRIX * dot_nt(back, right_pair[0])
        new_ref[part, :] = new
        copy_ref[part, :] = new.astype(BF)
        yield


def update_kernel(
    together,
    grad_ref, weight_ref, first_ref, second_ref, left_ref, right_ref,
    grad_out_ref, new_ref, copy_ref, first_new_ref, second_new_ref, left_new_ref, right_new_ref,
    left_base, right_base, left_rest, right_rest, move_ref,
):
    chains = []
    misses = []
    for which in range(together):
        grad = grad_ref[which]
        width = weight_ref.shape[2]
        if grad.shape[1] != width:
            height = weight_ref.shape[1]
            grad = jnp.concatenate([grad[at:at + height] for at in range(0, grad.shape[0], height)], axis=1)
        grad_out_ref[which] = grad.astype(F32)
        left = left_ref[which]
        right = right_ref[which]
        left_pair = split(left)
        right_pair = split(right)
        gram = dot_nt(grad, grad)
        pace = TURN_RATE / (jnp.sqrt(jnp.sum(gram * gram)) + 1e-06)
        left_base[which] = left + dot_nn(gram.astype(BF), left_pair[0]) * pace
        right_base[which] = right + dot_tn(grad, dot_nn(grad, right_pair[0]).astype(BF)) * pace
        misses.append(([], []))
        chains.append(renew_chain(right_base.at[which], right_new_ref.at[which], right_rest.at[which], misses[which][1]))
        chains.append(renew_chain(left_base.at[which], left_new_ref.at[which], left_rest.at[which], misses[which][0]))
        chains.append(
            move_chain(
                grad, left_pair, right_pair, weight_ref.at[which], first_ref.at[which], second_ref.at[which],
                new_ref.at[which], copy_ref.at[which], first_new_ref.at[which], second_new_ref.at[which],
                move_ref.at[which],
            )
        )
    in_step(chains)
    for which in range(together):
        for missed, base, out, rest in zip(
            misses[which], (left_base, right_base), (left_new_ref, right_new_ref), (left_rest, right_rest)
        ):
            worst = functools.reduce(jnp.maximum, missed)

            @pl.when(jnp.logical_not(worst < NEAR))
            def _(base=base, out=out, rest=rest):
                renew_rows(base.at[which], out.at[which], rest.at[which])


def update_stack(grad, skip, together, weight, first, second, left, right):
    slots, rows, width = weight.shape

    def spec(shape):
        return pl.BlockSpec((together,) + shape, lambda slot: (slot, 0, 0))

    flat = spec((rows, width))
    return pl.pallas_call(
        functools.partial(update_kernel, together),
        grid=(slots // together,),
        in_specs=[pl.BlockSpec((together,) + grad.shape[1:], lambda slot: (skip // together + slot, 0, 0))]
        + [flat] * 3 + [spec((rows, rows)), spec((width, width))],
        out_specs=[flat] * 5 + [spec((rows, rows)), spec((width, width))],
        out_shape=[
            jax.ShapeDtypeStruct(weight.shape, F32),
            jax.ShapeDtypeStruct(weight.shape, F32),
            jax.ShapeDtypeStruct(weight.shape, BF),
            jax.ShapeDtypeStruct(weight.shape, F32),
            jax.ShapeDtypeStruct(weight.shape, F32),
            jax.ShapeDtypeStruct(left.shape, F32),
            jax.ShapeDtypeStruct(right.shape, F32),
        ],
        scratch_shapes=[
            pltpu.VMEM((together, rows, rows), F32),
            pltpu.VMEM((together, width, width), F32),
            pltpu.VMEM((together, rows, rows), F32),
            pltpu.VMEM((together, width, width), F32),
            pltpu.VMEM((together, rows, width), BF),
        ],
        compiler_params=pltpu.CompilerParams(vmem_limit_bytes=60 * 1024 * 1024),
        name="rotated_update_%d" % width,
    )(grad, weight, first, second, left, right)


MESH = pl.DeviceIdType.MESH
P_SIZE = 197
NBR = 8
HEAD = 64
ROWS = 208
FAR = 200
CHUNK = 256
RADIX = 4
PARTS = 3


def layer_norm(values, gain, shift):
    centre = values - jnp.mean(values, axis=-1, keepdims=True)
    scale = lax.rsqrt(jnp.mean(centre * centre, axis=-1, keepdims=True) + 1e-06)
    normal = centre * scale
    return (normal * gain + shift, normal, scale)


def norm_back(grad, normal, scale, gain):
    shaped = grad * gain
    return scale * (
        shaped
        - jnp.mean(shaped, axis=-1, keepdims=True)
        - normal * jnp.mean(shaped * normal, axis=-1, keepdims=True)
    )


def gelu_pair(value):
    size = jnp.abs(value) * (1.0 / math.sqrt(2.0))
    bell = jnp.exp(-0.5 * value * value)
    part = 1.0 / (1.0 + 0.3275911 * size)
    series = part * (
        0.254829592
        + part * (-0.284496736 + part * (1.421413741 + part * (-1.453152027 + part * 1.061405429)))
    )
    tail = 0.5 * series * bell
    share = jnp.where(value < 0.0, tail, 1.0 - tail)
    return value * share, share + value * bell * (1.0 / math.sqrt(2.0 * math.pi))


def remote(src, dst, send, recv, device):
    return pltpu.make_async_remote_copy(
        src_ref=src, dst_ref=dst, send_sem=send, recv_sem=recv, device_id=device, device_id_type=MESH
    )


def block_kernel(
    chips, images,
    index_ref, valid_ref,
    tokens_ref, cotangent_ref, queue_ref, norms_ref, attn_own, mlp_own,
    out_ref, input_grad_ref, done, norm_out,
    attn_ref, mlp_ref,
    asked, parts_out, given, far_f,
    wide, tokens_f, normed, normal_one, scale_one, query, key, value, probs, mixed,
    middle, normal_two, scale_two, normed_two, cot_low, made,
    mlp_mine, mlp_away, square, both_out, both_grad,
    total, first_send, first_recv, sent, recv, norm_sum, norm_pair, norm_slots,
    ask_send, ask_recv, give_send, give_recv, swap_send, swap_recv,
    first_s, first_r, step_s, step_r, spread_s, spread_r, norm_s, norm_r, join_s, join_r,
):
    me = lax.axis_index("dp")
    core = lax.axis_index("mp")
    other = 1 - core
    count = tokens_ref.shape[0]
    width = tokens_ref.shape[1]
    depth = queue_ref.shape[0]
    picks = images * NBR
    pairs = width // (2 * HEAD)
    bits = chips.bit_length() - 1
    height = done.shape[1]
    grad_two = tokens_f
    grad_query, grad_key, grad_value, grad_mid_low = query, key, value, normed_two

    barrier = pltpu.get_barrier_semaphore()
    pl.semaphore_signal(barrier, inc=1, device_id=(me, other), device_id_type=MESH)

    def greet(hop, carry):
        pl.semaphore_signal(
            barrier, inc=1, device_id=(lax.rem(me + hop, chips), core), device_id_type=MESH
        )
        return carry

    lax.fori_loop(1, chips, greet, 0)
    pick_row = lax.broadcasted_iota(jnp.int32, (picks, depth), 0)
    wanted = jnp.zeros((picks, depth), jnp.int32)
    for pick in range(picks):
        wanted = jnp.where(
            pick_row == pick, index_ref[core * images + pick // NBR, pick % NBR], wanted
        )
    asked[0] = wanted
    attn_ref[:, core] = attn_own[...].astype(BF)
    mlp_ref[:, core] = mlp_own[...].astype(BF)
    pl.semaphore_wait(barrier, chips)

    def ask(hop):
        return remote(
            asked.at[0], asked.at[hop], ask_send.at[hop], ask_recv.at[hop],
            (lax.rem(me + hop, chips), core),
        )

    def give(hop):
        return remote(
            parts_out.at[hop], given.at[hop], give_send.at[hop], give_recv.at[hop],
            (lax.rem(me + chips - hop, chips), core),
        )

    def start_ask(hop, carry):
        ask(hop).start()
        return carry

    lax.fori_loop(1, chips, start_ask, 0)
    swaps = [
        remote(ref.at[:, core], ref.at[:, core], swap_send.at[place], swap_recv.at[place], (me, other))
        for place, ref in enumerate((attn_ref, mlp_ref))
    ]
    for swap in swaps:
        swap.start()

    def spread(source, target):
        for which in range(count // (images * P_SIZE)):

            @pl.when(core == which)
            def _(which=which):
                for image in range(images):
                    start = (which * images + image) * P_SIZE
                    target[image * ROWS:(image + 1) * ROWS, :] = source[start:start + ROWS, :]

    wide[:count, :] = tokens_ref[...].astype(F32)
    wide[count:, :] = jnp.zeros((wide.shape[0] - count, width), F32)
    spread(wide, tokens_f)

    places = lax.broadcasted_iota(jnp.int32, (picks, depth), 1) + me * depth

    def choose(wish):
        chooser = jnp.where(wish == places, 1.0, 0.0).astype(BF)
        return dot_nn(chooser, queue_ref[...]).astype(BF)

    def answer(hop, carry):
        ask(hop).wait_recv()
        parts_out[hop] = choose(asked[hop])
        give(hop).start()
        return carry

    lax.fori_loop(1, chips, answer, 0)
    given[0] = choose(wanted)
    wide[:count, :] = cotangent_ref[...].astype(F32)
    spread(wide, made)
    own_row = lax.broadcasted_iota(jnp.int32, (ROWS, 1), 0) < P_SIZE
    lane = lax.broadcasted_iota(jnp.int32, (1, 2 * HEAD), 1)
    first_head = lane < HEAD
    key_lane = lax.broadcasted_iota(jnp.int32, (1, ROWS), 1)

    def halves(pair):
        zero = jnp.zeros_like(pair)
        return jnp.where(first_head, pair, zero), jnp.where(first_head, zero, pair)

    def place_of(image):
        return pl.ds(pl.multiple_of(image * ROWS, ROWS), ROWS)

    def step_norm(image, carry):
        here = place_of(image)
        cot_low[here, :] = jnp.where(own_row, made[here, :], 0.0).astype(BF)
        normed_f, normal, scale = layer_norm(tokens_f[here, :], norms_ref[0:1, :], norms_ref[1:2, :])
        normal_one[here, :] = normal
        scale_one[here, :] = scale
        made[here, :] = jnp.where(own_row, normed_f, 0.0)
        return carry

    lax.fori_loop(0, images, step_norm, 0)

    def collect(hop, sums):
        give(hop).wait_recv()
        return sums + given[hop].astype(F32)

    far_f[...] = lax.fori_loop(1, chips, collect, given[0].astype(F32))
    for swap in swaps:
        swap.wait_recv()

    def weight(slot):
        return attn_ref[slot].reshape(width, width)

    def step_forward(image, carry):
        here = place_of(image)
        x = tokens_f[here, :]
        far = far_f[pl.ds(pl.multiple_of(image * NBR, NBR), NBR), :]
        full = jnp.concatenate([made[here, :][:FAR, :], far], axis=0).astype(BF)
        normed[here, :] = full
        q = dot_nt(full, weight(0)).astype(BF)
        k = dot_nt(full, weight(1)).astype(BF)
        v = dot_nt(full, weight(2)).astype(BF)
        query[here, :] = q
        key[here, :] = k
        value[here, :] = v
        bias = jnp.where(key_lane < P_SIZE, 0.0, -1e30)
        for slot in range(NBR):
            okay = valid_ref[core * images + image, slot] > 0
            bias = jnp.where(key_lane == FAR + slot, jnp.where(okay, 0.0, -1e30), bias)
        parts = []
        for pair in range(pairs):
            cols = slice(pair * 2 * HEAD, (pair + 1) * 2 * HEAD)
            k_pair = k[:, cols]
            sums = 0.0
            for head, (q_one, v_one) in enumerate(zip(halves(q[:, cols]), halves(v[:, cols]))):
                scores = dot_nt(q_one, k_pair) * 0.125 + bias
                top = jnp.max(scores, axis=-1, keepdims=True)
                powers = jnp.exp(scores - top)
                prob = powers / jnp.sum(powers, axis=-1, keepdims=True)
                probs[image * 2 * pairs + 2 * pair + head] = prob
                sums = sums + dot_nn(prob.astype(BF), v_one)
            parts.append(sums.astype(BF))
        mix = jnp.concatenate(parts, axis=1)
        mixed[here, :] = mix
        mid = x + dot_nn(mix, weight(3))
        middle[here, :] = mid
        two_f, normal, scale = layer_norm(mid, norms_ref[2:3, :], norms_ref[3:4, :])
        normal_two[here, :] = normal
        scale_two[here, :] = scale
        normed_two[here, :] = two_f.astype(BF)
        return carry

    lax.fori_loop(0, images, step_forward, 0)

    made[...] = jnp.zeros_like(made)
    grad_two[...] = jnp.zeros_like(grad_two)
    chunks = mlp_ref.shape[3] // CHUNK

    def step_mlp(half, target):
        def step(turn, carry):
            cols = pl.ds(pl.multiple_of(turn * CHUNK, CHUNK), CHUNK)
            w_one = mlp_ref[0, half, :, cols]
            w_two = mlp_ref[1, half, :, cols]
            two = normed_two[...]
            cot = cot_low[...]
            hidden, slope = gelu_pair(dot_nn(two, w_one))
            hidden = hidden.astype(BF)
            grad_inner = (dot_nn(cot, w_two) * slope).astype(BF)
            made[...] += dot_nt(hidden, w_two)
            grad_two[...] += dot_nt(grad_inner, w_one)
            target[0, :, cols] = dot_tn(two, grad_inner).astype(target.dtype)
            target[1, :, cols] = dot_tn(cot, hidden).astype(target.dtype)
            return carry

        lax.fori_loop(0, chunks, step, 0)

    lo = me % RADIX
    hi = me // RADIX % RADIX
    peers = (lambda hop: me - lo + (lo + hop) % RADIX, lambda hop: me - RADIX * hi + RADIX * ((hi + hop) % RADIX))
    digits = (lo, hi)
    plan = ((0, 1), (1, 0), (0, 1))
    quarter, shard = height // RADIX, height // RADIX**2
    extra = list(range(4, bits))
    pending = []
    waits = [[] for unused in range(PARTS)]

    def send(part, src, dst, pair, device):
        copy = remote(src, dst, pair[0], pair[1], device)
        copy.start()
        pending.append(copy)
        waits[part].append(copy)

    def arrived(part):
        for copy in waits[part]:
            copy.wait_recv()
        waits[part].clear()

    def rows(start, size):
        return pl.ds(pl.multiple_of(start, 16), size)

    def copy_blocks(target, source, part):
        tall = source.shape[1]
        for block in range(source.shape[2] // width):
            target[part, block * tall:(block + 1) * tall, :] = source[
                part, :, block * width:(block + 1) * width
            ]

    def begin(part):
        send(part, first_send.at[part], first_recv.at[part], (first_s.at[part], first_r.at[part]), (me, other))

    def reduce_one(part):
        arrived(part)
        axis = plan[part][0]
        for hop in range(1, RADIX):
            away = rows((digits[axis] + hop) % RADIX * quarter, quarter)
            slot = pl.ds((hop - 1) * quarter, quarter)
            sent[part, slot, :] = (total[part, away, :] + first_recv[part, away, :].astype(F32)).astype(BF)
            send(
                part, sent.at[part, slot], recv.at[part, slot],
                (step_s.at[part, hop - 1], step_r.at[part, hop - 1]), (peers[axis](hop), core),
            )
        held = rows(digits[axis] * quarter, quarter)
        total[part, held, :] += first_recv[part, held, :].astype(F32)

    def reduce_two(part):
        arrived(part)
        first, second = plan[part]
        start = digits[first] * quarter

        def summed(at, size):
            sums = total[part, rows(start + at, size), :]
            for hop in range(1, RADIX):
                sums = sums + recv[part, rows((hop - 1) * quarter + at, size), :].astype(F32)
            return sums

        base = (RADIX - 1) * quarter
        for hop in range(1, RADIX):
            slot = pl.ds(base + (hop - 1) * shard, shard)
            sent[part, slot, :] = summed((digits[second] + hop) % RADIX * shard, shard).astype(BF)
            send(
                part, sent.at[part, slot], recv.at[part, slot],
                (step_s.at[part, RADIX - 2 + hop], step_r.at[part, RADIX - 2 + hop]),
                (peers[second](hop), core),
            )
        at = digits[second] * shard
        total[part, rows(start + at, shard), :] = summed(at, shard)

    def spread_one(part):
        arrived(part)
        first, second = plan[part]
        start = digits[first] * quarter + digits[second] * shard
        held = rows(start, shard)
        sums = total[part, held, :]
        base = (RADIX - 1) * quarter
        for hop in range(1, RADIX):
            sums = sums + recv[part, pl.ds(base + (hop - 1) * shard, shard), :].astype(F32)
        base = base + (RADIX - 1) * shard
        for turn, bit in enumerate(extra):
            slot = pl.ds(base + turn * shard, shard)
            sent[part, slot, :] = sums.astype(BF)
            mate = me + (1 - 2 * (me // 2**bit % 2)) * 2**bit
            at = 2 * (RADIX - 1) + turn
            send(part, sent.at[part, slot], recv.at[part, slot], (step_s.at[part, at], step_r.at[part, at]), (mate, core))
            arrived(part)
            sums = sent[part, slot, :].astype(F32) + recv[part, slot, :].astype(F32)
        done[part, held, :] = sums.astype(BF)
        for hop in range(1, RADIX):
            send(
                part, done.at[part, held], done.at[part, held],
                (spread_s.at[part, hop - 1], spread_r.at[part, hop - 1]), (peers[second](hop), core),
            )

    def spread_two(part):
        arrived(part)
        axis = plan[part][0]
        held = rows(digits[axis] * quarter, quarter)
        for hop in range(1, RADIX):
            send(
                part, done.at[part, held], done.at[part, held],
                (spread_s.at[part, RADIX - 2 + hop], spread_r.at[part, RADIX - 2 + hop]),
                (peers[axis](hop), core),
            )

    step_mlp(other, mlp_away)
    for part in range(2):
        copy_blocks(first_send, mlp_away, part)
        begin(part)
    step_mlp(core, mlp_mine)
    for part in range(2):
        copy_blocks(total, mlp_mine, part)
        reduce_one(part)

    norm_sum[...] = jnp.zeros_like(norm_sum)

    def step_backward(image, carry):
        here = place_of(image)
        made[here, :] += middle[here, :]
        both_out[core, here, :] = made[here, :].astype(BF)
        grad_n = grad_two[here, :]
        normal = normal_two[here, :]
        norm_sum[2:3, :] += jnp.sum(grad_n * normal, axis=0, keepdims=True)
        norm_sum[3:4, :] += jnp.sum(grad_n, axis=0, keepdims=True)
        grad_mid = cot_low[here, :].astype(F32) + norm_back(
            grad_n, normal, scale_two[here, :], norms_ref[2:3, :]
        )
        low = grad_mid.astype(BF)
        grad_mid_low[here, :] = low
        grad_mix = dot_nt(low, weight(3)).astype(BF)
        q = query[here, :]
        k = key[here, :]
        v = value[here, :]
        parts_q, parts_k, parts_v = [], [], []
        for pair in range(pairs):
            cols = slice(pair * 2 * HEAD, (pair + 1) * 2 * HEAD)
            gm_pair = grad_mix[:, cols]
            sum_q = sum_k = sum_v = 0.0
            for head, (q_one, k_one, v_one, gm_one) in enumerate(
                zip(halves(q[:, cols]), halves(k[:, cols]), halves(v[:, cols]), halves(gm_pair))
            ):
                prob = probs[image * 2 * pairs + 2 * pair + head]
                grad_prob = dot_nt(gm_pair, v_one)
                sum_v = sum_v + dot_tn(prob.astype(BF), gm_one)
                weighed = prob * grad_prob
                grad_score = (
                    weighed - prob * jnp.sum(weighed, axis=-1, keepdims=True)
                ).astype(BF)
                sum_q = sum_q + dot_nn(grad_score, k_one)
                sum_k = sum_k + dot_tn(grad_score, q_one)
            parts_q.append((sum_q * 0.125).astype(BF))
            parts_k.append((sum_k * 0.125).astype(BF))
            parts_v.append(sum_v.astype(BF))
        gq = jnp.concatenate(parts_q, axis=1)
        gk = jnp.concatenate(parts_k, axis=1)
        gv = jnp.concatenate(parts_v, axis=1)
        grad_query[here, :] = gq
        grad_key[here, :] = gk
        grad_value[here, :] = gv
        grad_n = dot_nn(gq, weight(0)) + dot_nn(gk, weight(1)) + dot_nn(gv, weight(2))
        grad_n = jnp.where(own_row, grad_n, 0.0)
        normal = normal_one[here, :]
        norm_sum[0:1, :] += jnp.sum(grad_n * normal, axis=0, keepdims=True)
        norm_sum[1:2, :] += jnp.sum(grad_n, axis=0, keepdims=True)
        both_grad[core, here, :] = grad_mid + norm_back(
            grad_n, normal, scale_one[here, :], norms_ref[0:1, :]
        )
        return carry

    lax.fori_loop(0, images // 2, step_backward, 0)
    for part in range(2):
        reduce_two(part)
    lax.fori_loop(images // 2, images, step_backward, 0)

    def norm_send(src, dst, place, device):
        copy = remote(src, dst, norm_s.at[place], norm_r.at[place], device)
        copy.start()
        pending.append(copy)
        return copy

    norm_pair[core] = norm_sum[...]
    norm_wait = [norm_send(norm_pair.at[core], norm_pair.at[core], 0, (me, other))]
    joins = [
        remote(ref.at[core], ref.at[core], join_s.at[place], join_r.at[place], (me, other))
        for place, ref in enumerate((both_out, both_grad))
    ]
    for join in joins:
        join.start()

    tall = attn_own.shape[1]
    for slot, (left, right) in enumerate(
        ((grad_query, normed), (grad_key, normed), (grad_value, normed), (mixed, grad_mid_low))
    ):
        square[...] = dot_tn(left[...], right[...])
        place = pl.ds(slot * tall, tall)
        first_send[2, place, :] = square[rows(other * tall, tall), :].astype(BF)
        total[2, place, :] = square[rows(core * tall, tall), :]
    begin(2)
    for part in range(2):
        spread_one(part)
    reduce_one(2)

    norm_wait[0].wait_recv()
    norm_sum[...] = norm_pair[0] + norm_pair[1]
    norm_slots[0, lo] = norm_sum[...]
    norm_wait = [
        norm_send(norm_slots.at[0, lo], norm_slots.at[0, lo], hop, (peers[0](hop), core))
        for hop in range(1, RADIX)
    ]
    for part in range(2):
        spread_two(part)
    reduce_two(2)

    for one in norm_wait:
        one.wait_recv()
    norm_sum[...] = (norm_slots[0, 0] + norm_slots[0, 1]) + (norm_slots[0, 2] + norm_slots[0, 3])
    norm_slots[1, hi] = norm_sum[...]
    norm_wait = [
        norm_send(norm_slots.at[1, hi], norm_slots.at[1, hi], RADIX - 1 + hop, (peers[1](hop), core))
        for hop in range(1, RADIX)
    ]
    spread_one(2)

    for join in joins:
        join.wait_recv()
    wide[...] = jnp.zeros_like(wide)
    for image in range(count // P_SIZE):
        which, at = image // images, image % images * ROWS
        span = slice(image * P_SIZE, (image + 1) * P_SIZE)
        wide[span, :] = both_out[which, at:at + ROWS, :].astype(F32)[:P_SIZE, :]
        input_grad_ref[span, :] = both_grad[which, at:at + P_SIZE, :]
    out_ref[...] = wide[:count, :].astype(BF)

    for one in norm_wait:
        one.wait_recv()
    norm_sum[...] = (norm_slots[1, 0] + norm_slots[1, 1]) + (norm_slots[1, 2] + norm_slots[1, 3])
    for turn, bit in enumerate(extra):
        mate = me + (1 - 2 * (me // 2**bit % 2)) * 2**bit
        norm_slots[2 + turn, 0] = norm_sum[...]
        norm_send(norm_slots.at[2 + turn, 0], norm_slots.at[2 + turn, 1], 2 * RADIX - 1 + turn, (mate, core)).wait_recv()
        norm_sum[...] = norm_slots[2 + turn, 0] + norm_slots[2 + turn, 1]
    norm_out[...] = norm_sum[...]

    spread_two(2)
    for part in range(PARTS):
        arrived(part)
    for one in pending + joins + swaps:
        one.wait_send()

    def finish(hop, carry):
        ask(hop).wait_send()
        give(hop).wait_send()
        return carry

    lax.fori_loop(1, chips, finish, 0)


def block(chips, nbr_index, nbr_valid, tokens, cotangent, queue, norms, attn, mlp):
    count, width = tokens.shape
    cores = width // attn.shape[1]
    images = nbr_valid.shape[0] // cores
    tall = images * ROWS
    padded = count + 16 - count % 8
    heads = width // HEAD
    picks = images * NBR
    bits = chips.bit_length() - 1
    extra = max(0, bits - 4)
    height = attn.shape[0] * attn.shape[1]
    quarter, shard = height // RADIX, height // RADIX**2
    moving = (RADIX - 1) * (quarter + shard) + extra * shard
    vmem = pl.BlockSpec(memory_space=pltpu.VMEM)
    smem = pl.BlockSpec(memory_space=pltpu.SMEM)
    dma = pltpu.SemaphoreType.DMA
    flat_f = pltpu.VMEM((tall, width), F32)
    flat_low = pltpu.VMEM((tall, width), BF)
    column = pltpu.VMEM((tall, 1), F32)
    steps = 2 * (RADIX - 1)
    return pl.pallas_call(
        functools.partial(block_kernel, chips, images),
        in_specs=[smem] * 2 + [vmem] * 6,
        out_specs=[vmem] * 4,
        out_shape=[
            jax.ShapeDtypeStruct((count, width), BF),
            jax.ShapeDtypeStruct((count, width), F32),
            jax.ShapeDtypeStruct((PARTS, height, width), BF),
            jax.ShapeDtypeStruct(norms.shape, F32),
        ],
        scratch_shapes=[
            pltpu.VMEM((attn.shape[0], cores) + attn.shape[1:], BF),
            pltpu.VMEM((mlp.shape[0], cores) + mlp.shape[1:], BF),
            pltpu.VMEM((chips, picks, queue.shape[0]), jnp.int32),
            pltpu.VMEM((chips, picks, width), BF),
            pltpu.VMEM((chips, picks, width), BF),
            pltpu.VMEM((picks, width), F32),
            pltpu.VMEM((padded, width), F32),
            flat_f, flat_low, flat_f, column, flat_low, flat_low, flat_low,
            pltpu.VMEM((images * heads, ROWS, ROWS), F32),
            flat_low,
            flat_f, flat_f, column, flat_low, flat_low, flat_f,
            pltpu.VMEM(mlp.shape, F32),
            pltpu.VMEM(mlp.shape, BF),
            pltpu.VMEM((width, width), F32),
            pltpu.VMEM((cores, tall, width), BF),
            pltpu.VMEM((cores, tall, width), F32),
            pltpu.VMEM((PARTS, height, width), F32),
            pltpu.VMEM((PARTS, height, width), BF),
            pltpu.VMEM((PARTS, height, width), BF),
            pltpu.VMEM((PARTS, moving, width), BF),
            pltpu.VMEM((PARTS, moving, width), BF),
            pltpu.VMEM(norms.shape, F32),
            pltpu.VMEM((cores,) + norms.shape, F32),
            pltpu.VMEM((2 + extra, RADIX) + norms.shape, F32),
            dma((chips,)), dma((chips,)), dma((chips,)), dma((chips,)),
            dma((2,)), dma((2,)),
            dma((PARTS,)), dma((PARTS,)),
            dma((PARTS, steps + extra)), dma((PARTS, steps + extra)),
            dma((PARTS, steps)), dma((PARTS, steps)),
            dma((steps + 1 + extra,)), dma((steps + 1 + extra,)),
            dma((2,)), dma((2,)),
        ],
        compiler_params=pltpu.CompilerParams(
            collective_id=0, has_side_effects=True, vmem_limit_bytes=62 * 1024 * 1024
        ),
        name="block_both_ways",
    )(nbr_index, nbr_valid, tokens, cotangent, queue, norms, attn, mlp)


RATE_NORM = 0.6


def body(
    chips,
    tokens,
    cotangent,
    queue,
    nbr_index,
    nbr_valid,
    norm_params,
    norm_first,
    norm_second,
    attn_weight,
    mlp_weight,
    attn_first,
    attn_second,
    mlp_first,
    mlp_second,
    attn_left,
    attn_right,
    mlp_left,
    mlp_right,
):
    def flip(value):
        return value.transpose(0, 2, 1)

    attn_own = flip(attn_weight)
    block_out, input_grad, summed, norm_grad = block(
        chips, nbr_index, nbr_valid, tokens, cotangent, queue, norm_params, attn_own, mlp_weight
    )
    norm_first_new = BETA_FIRST * norm_first + (1.0 - BETA_FIRST) * norm_grad
    norm_second_new = BETA_SECOND * norm_second + (1.0 - BETA_SECOND) * norm_grad * norm_grad
    norm_new = norm_params - RATE_NORM * (norm_first_new / (1.0 - BETA_FIRST**STEP)) / (
        jnp.sqrt(norm_second_new / (1.0 - BETA_SECOND**STEP)) + EPSILON
    )
    slots, rows, width = attn_own.shape
    (
        mlp_grad,
        mlp_new,
        mlp_copy,
        mlp_first_new,
        mlp_second_new,
        mlp_left_new,
        mlp_right_new,
    ) = update_stack(
        summed, 0, 1, mlp_weight, mlp_first, mlp_second, mlp_left, mlp_right
    )
    (
        attn_grad,
        attn_new,
        attn_copy,
        attn_first_new,
        attn_second_new,
        attn_right_new,
        attn_left_new,
    ) = update_stack(
        summed.reshape(-1, rows, width),
        2 * slots,
        2,
        attn_own,
        flip(attn_first),
        flip(attn_second),
        attn_right,
        attn_left,
    )
    return (
        block_out,
        input_grad,
        norm_grad,
        flip(attn_grad),
        mlp_grad,
        norm_first_new,
        norm_second_new,
        norm_new,
        flip(attn_first_new),
        flip(attn_second_new),
        mlp_first_new,
        mlp_second_new,
        attn_left_new,
        attn_right_new,
        mlp_left_new,
        mlp_right_new,
        flip(attn_new),
        flip(attn_copy),
        mlp_new,
        mlp_copy,
    )


def solution(mesh):
    return jax.shard_map(
        functools.partial(body, mesh.shape["dp"]),
        mesh=mesh,
        in_specs=(
            P("dp", None),
            P("dp", None),
            P("dp", None),
            P("dp", None),
            P("dp", None),
            P(),
            P(),
            P(),
            P(None, None, "mp"),
            P(None, None, "mp"),
            P(None, None, "mp"),
            P(None, None, "mp"),
            P(None, None, "mp"),
            P(None, None, "mp"),
            P(None, "mp", None),
            P(None, "mp", None),
            P(None, "mp", None),
            P(None, "mp", None),
        ),
        out_specs=(
            P("dp", None),
            P("dp", None),
            P(),
            P(None, None, "mp"),
            P(None, None, "mp"),
            P(),
            P(),
            P(),
            P(None, None, "mp"),
            P(None, None, "mp"),
            P(None, None, "mp"),
            P(None, None, "mp"),
            P(None, "mp", None),
            P(None, "mp", None),
            P(None, "mp", None),
            P(None, "mp", None),
            P(None, None, "mp"),
            P(None, None, "mp"),
            P(None, None, "mp"),
            P(None, None, "mp"),
        ),
        check_vma=False,
    )
```

time: 218 us -> 183 us (0.84); the launches traced: 218 us -> 180 us
  Pallas kernels: 191 us -> 176 us
  between operations: 14.2 us -> 0.93 us
  local copies, waits for them, and re-layouts: 10.6 us -> 3.21 us
    pallas_call x3 -> x1, Pallas kernels: 129 us -> 103 us  [block(): pl.pallas_call(functools.partial(block_kernel, chips, images), in_specs=[...]
    pallas_call x2, Pallas kernels: 62.3 us -> 72.8 us  [update_stack(): pl.pallas_call(functools.partial(update_kernel, together), grid=(slots //...]
    unnamed x23 -> x15, local copies, waits for them, and re-layouts: 9.81 us -> 3.21 us
  transfers between devices with their start and end apart: 2 -> 0, of which waited for: 0 -> 0; matrix products, arithmetic and copies ran while one was open for 0% -> 0% of each run, Pallas kernels for 58% -> 0%
where the time goes in v1:
time: 183 us; the launch traced here: 180 us
  Pallas kernels  176 us (96%)
  local copies, waits for them, and re-layouts  3.21 us (2%)
    pallas_call x1, Pallas kernels, block(): pl.pallas_call(functools.partial(block_kernel, chips, images), in_specs=[...  103 us
    pallas_call x2, Pallas kernels, update_stack(): pl.pallas_call(functools.partial(update_kernel, together), grid=(slots //...  72.8 us

profile of v1, /device:TPU:0, one launch (start us, length us, event | category | flops | bytes accessed | tf_op | source)
XLA Modules:
  0.0 180.3 jit_solution(3889359515073861371)
XLA Ops:
  0.7 102.8 %block_both_ways.1 = (bf16[1576,384]{1,0:T(8,128)(2,1)}, f32[1576,384]{1,0:T(8,128)}, bf16[3,768,384]{2,1,0:T(8,128)(2,1)}, f32[4,384]{1,0:T(4,128)}) custom-call(s32[8,8]{1,0:T(8,128)} %index_ref.1, s32[8,8]{1,0:T(8,128)} %valid_ref.1, bf16[1576,384]{1,0:T(8,128)(2,1)} %tokens_ref.1, bf16[1576,384]{1,0:T(8,128)(2,1)} %cotangent_ref.1, ...), custom_call_target="tpu_custom_call" | custom-call | tf_op jit(solution)/shard_map/block_both_ways/pallas_call | solution.py:772
  103.5 22.4 %rotated_update_384.1 = (f32[4,192,384]{2,1,0:T(8,128)}, f32[4,192,384]{2,1,0:T(8,128)}, bf16[4,192,384]{2,1,0:T(8,128)(2,1)}, f32[4,192,384]{2,1,0:T(8,128)}, f...) custom-call(bf16[12,192,384]{2,1,0:T(8,128)(2,1)} %bitcast.9, f32[4,192,384]{2,1,0:T(8,128)} %bitcast.11, ...), custom_call_target="tpu_custom_call" | custom-call | tf_op jit(solution)/shard_map/rotated_update_384/pallas_call | solution.py:222
  125.9 0.0 copy-start.2
  125.9 0.0 copy-start.3
  125.9 0.0 copy-start.4
  125.9 0.0 copy-start.5
  126.0 0.0 copy-start.1
  126.0 50.3 %rotated_update_768.1 = (f32[2,384,768]{2,1,0:T(8,128)}, f32[2,384,768]{2,1,0:T(8,128)}, bf16[2,384,768]{2,1,0:T(8,128)(2,1)}, f32[2,384,768]{2,1,0:T(8,128)}, f...) custom-call(bf16[3,768,384]{2,1,0:T(8,128)(2,1)} %get-tuple-element.41.grad_ref, ...), custom_call_target="tpu_custom_call" | custom-call | tf_op jit(solution)/shard_map/rotated_update_768/pallas_call | solution.py:222
  176.3 0.0 copy-start
  176.3 0.0 copy-done.2
  176.3 0.0 copy-done.3
  176.3 0.0 copy-done.4
  176.3 0.0 copy-done.5
  176.3 0.6 divide_subtract_fusion
  177.0 0.0 copy-done.1
  177.0 1.0 copy.41
  178.0 0.1 copy-done
  178.1 1.4 copy.42
  179.6 0.6 copy.43
Async XLA Ops:
  125.9 50.4 %copy-start.2 = (f32[4,384]{1,0:T(4,128)S(1)}, f32[4,384]{1,0:T(4,128)}, u32[]{:S(2)}) copy-start(f32[4,384]{1,0:T(4,128)} %norms_ref.1) | copy-start | bytes 18436
  125.9 50.4 %copy-start.3 = (f32[4,384]{1,0:T(4,128)S(1)}, f32[4,384]{1,0:T(4,128)}, u32[]{:S(2)}) copy-start(f32[4,384]{1,0:T(4,128)} %get-tuple-element.81) | copy-start | bytes 18436
  125.9 50.4 %copy-start.4 = (f32[4,384]{1,0:T(4,128)S(1)}, f32[4,384]{1,0:T(4,128)}, u32[]{:S(2)}) copy-start(f32[4,384]{1,0:T(4,128)} %param.25) | copy-start | bytes 18436
  125.9 50.4 %copy-start.5 = (f32[4,384]{1,0:T(4,128)S(1)}, f32[4,384]{1,0:T(4,128)}, u32[]{:S(2)}) copy-start(f32[4,384]{1,0:T(4,128)} %param.24) | copy-start | bytes 18436
  126.0 51.0 %copy-start.1 = (bf16[1576,384]{1,0:T(8,128)(2,1)S(1)}, bf16[1576,384]{1,0:T(8,128)(2,1)}, u32[]{:S(2)}) copy-start(bf16[1576,384]{1,0:T(8,128)(2,1)} %get-tuple-element.79) | copy-start | bytes 3631108
  176.3 1.8 %copy-start = (f32[1576,384]{1,0:T(8,128)S(1)}, f32[1576,384]{1,0:T(8,128)}, u32[]{:S(2)}) copy-start(f32[1576,384]{1,0:T(8,128)} %get-tuple-element.80) | copy-start | bytes 7262212

commit v2 on v1

--- a/solution.py
+++ b/solution.py
@@ -19,6 +19,7 @@
 ROUNDS = 3
 NEAR = 0.01
 PIECE = 128
+PAUSES = 40
 
 BF = jnp.bfloat16
 F32 = jnp.float32
@@ -167,29 +168,199 @@
         yield
 
 
+RATE_NORM = 0.6
+
+
+MESH = pl.DeviceIdType.MESH
+RADIX = 4
+
+
+def remote(src, dst, send, recv, device):
+    return pltpu.make_async_remote_copy(
+        src_ref=src, dst_ref=dst, send_sem=send, recv_sem=recv, device_id=device, device_id_type=MESH
+    )
+
+
+def set_bases(grad, left, right, left_low, right_low, left_base, right_base):
+    gram = dot_nt(grad, grad)
+    pace = TURN_RATE / (jnp.sqrt(jnp.sum(gram * gram)) + 1e-06)
+    left_base[...] = left + dot_nn(gram.astype(BF), left_low) * pace
+    right_base[...] = right + dot_tn(grad, dot_nn(grad, right_low).astype(BF)) * pace
+
+
+def side_by_side(grad, height):
+    return jnp.concatenate([grad[at:at + height] for at in range(0, grad.shape[0], height)], axis=1)
+
+
+def spread_chain(chips, partial_ref, attn_grad, sent, recv, sems):
+    me = lax.axis_index("dp")
+    core = lax.axis_index("mp")
+    count = RADIX**2
+    seat = me % count
+    shard = partial_ref.shape[0]
+    spread_s, spread_r, extra_s, extra_r = sems
+    extra = list(range(4, chips.bit_length() - 1))
+    held = pl.ds(pl.multiple_of((seat % RADIX * RADIX + seat // RADIX) * shard, 16), shard)
+
+    def peer(hop):
+        return (me - seat + (seat + hop) % count, core)
+
+    def mate(bit):
+        return (me + (1 - 2 * (me // 2**bit % 2)) * 2**bit, core)
+
+    def spread(hop):
+        return remote(attn_grad.at[held], attn_grad.at[held], spread_s.at[hop], spread_r.at[hop], peer(hop))
+
+    barrier = pltpu.get_barrier_semaphore()
+
+    def greet(hop, carry):
+        pl.semaphore_signal(barrier, inc=1, device_id=peer(hop), device_id_type=MESH)
+        return carry
+
+    lax.fori_loop(1, count, greet, 0)
+    for bit in extra:
+        pl.semaphore_signal(barrier, inc=1, device_id=mate(bit), device_id_type=MESH)
+    yield
+    pl.semaphore_wait(barrier, count - 1 + len(extra))
+    sums = partial_ref[...]
+    for turn, bit in enumerate(extra):
+        sent[turn] = sums.astype(BF)
+        copy = remote(sent.at[turn], recv.at[turn], extra_s.at[turn], extra_r.at[turn], mate(bit))
+        copy.start()
+        copy.wait()
+        sums = sent[turn].astype(F32) + recv[turn].astype(F32)
+    attn_grad[held, :] = sums.astype(BF)
+
+    def start(hop, carry):
+        spread(hop).start()
+        return carry
+
+    lax.fori_loop(1, count, start, 0)
+    for unused in range(PAUSES):
+        yield
+
+    def finish(hop, carry):
+        spread(hop).wait()
+        return carry
+
+    lax.fori_loop(1, count, finish, 0)
+
+
+def turn_mlp_kernel(
+    chips, grad_ref, left_ref, right_ref, partial_ref,
+    left_new_ref, right_new_ref, miss_ref, attn_grad,
+    left_base, right_base, left_rest, right_rest, sent, recv, *sems,
+):
+    slots, rows = left_ref.shape[:2]
+    chains = [spread_chain(chips, partial_ref, attn_grad, sent, recv, sems)]
+    next(chains[0])
+    misses = []
+    for which in range(slots):
+        grad = side_by_side(grad_ref[which], rows)
+        left = left_ref[which]
+        right = right_ref[which]
+        set_bases(grad, left, right, left.astype(BF), right.astype(BF), left_base.at[which], right_base.at[which])
+        misses.append(([], []))
+        for side, (base, out, rest) in enumerate(
+            ((left_base, left_new_ref, left_rest), (right_base, right_new_ref, right_rest))
+        ):
+            chains.append(renew_chain(base.at[which], out.at[which], rest.at[which], misses[which][side]))
+    in_step(chains)
+    for which in range(slots):
+        for side in range(2):
+            miss_ref[which, side] = functools.reduce(jnp.maximum, misses[which][side])
+
+
+def turn_mlp(chips, grad, left, right, partial):
+    extra = max(0, chips.bit_length() - 1 - 4)
+    shard, width = partial.shape
+    vmem = pl.BlockSpec(memory_space=pltpu.VMEM)
+    like = jax.ShapeDtypeStruct
+    moving = pltpu.VMEM((max(1, extra), shard, width), BF)
+    peer_sems = pltpu.SemaphoreType.DMA((RADIX**2,))
+    extra_sems = pltpu.SemaphoreType.DMA((max(1, extra),))
+    return pl.pallas_call(
+        functools.partial(turn_mlp_kernel, chips),
+        in_specs=[vmem] * 4,
+        out_specs=[vmem, vmem, pl.BlockSpec(memory_space=pltpu.SMEM), vmem],
+        out_shape=[
+            like(left.shape, F32),
+            like(right.shape, F32),
+            like((left.shape[0], 2), F32),
+            like((RADIX**2 * shard, width), BF),
+        ],
+        scratch_shapes=[
+            pltpu.VMEM(left.shape, F32),
+            pltpu.VMEM(right.shape, F32),
+            pltpu.VMEM(left.shape, F32),
+            pltpu.VMEM(right.shape, F32),
+            moving,
+            moving,
+        ]
+        + [peer_sems] * 2
+        + [extra_sems] * 2,
+        compiler_params=pltpu.CompilerParams(
+            collective_id=1, has_side_effects=True, vmem_limit_bytes=60 * 1024 * 1024
+        ),
+        name="turn_mlp",
+    )(grad, left, right, partial)
+
+
 def update_kernel(
     together,
+    miss_ref, mlp_grad_ref, mlp_weight_ref, mlp_first_ref, mlp_second_ref, mlp_left_ref, mlp_right_ref,
     grad_ref, weight_ref, first_ref, second_ref, left_ref, right_ref,
+    norm_grad_ref, norm_ref, norm_first_ref, norm_second_ref,
+    mlp_left_made, mlp_right_made, block_ref, input_grad_ref,
+    mlp_grad_out, mlp_new_ref, mlp_copy_ref, mlp_first_new_ref, mlp_second_new_ref,
     grad_out_ref, new_ref, copy_ref, first_new_ref, second_new_ref, left_new_ref, right_new_ref,
-    left_base, right_base, left_rest, right_rest, move_ref,
+    norm_grad_out, norm_new, norm_first_new, norm_second_new,
+    mlp_left_out, mlp_right_out, block_out, input_grad_out,
+    mlp_move, left_base, right_base, left_rest, right_rest, move_ref, left_held, right_held, work,
+    block_held, input_grad_held, sems_in, sems_out,
 ):
+    slot = pl.program_id(0)
+    last = pl.num_programs(0) - 1
+
+    def copies(passed, at):
+        return (
+            [pltpu.make_async_copy(src, held, sems_in.at[at + place]) for place, (src, held, dst) in enumerate(passed)],
+            [pltpu.make_async_copy(held, dst, sems_out.at[at + place]) for place, (src, held, dst) in enumerate(passed)],
+        )
+
+    bases = copies(
+        ((mlp_left_made.at[slot], left_held, mlp_left_out.at[slot]), (mlp_right_made.at[slot], right_held, mlp_right_out.at[slot])), 0
+    )
+    wide = copies(((block_ref, block_held, block_out), (input_grad_ref, input_grad_held, input_grad_out)), 2)
+
+    @pl.when(slot == 0)
+    def _():
+        for copy in wide[0]:
+            copy.start()
+        grad = norm_grad_ref[...]
+        first = BETA_FIRST * norm_first_ref[...] + (1.0 - BETA_FIRST) * grad
+        second = BETA_SECOND * norm_second_ref[...] + (1.0 - BETA_SECOND) * grad * grad
+        norm_grad_out[...] = grad
+        norm_first_new[...] = first
+        norm_second_new[...] = second
+        norm_new[...] = norm_ref[...] - RATE_NORM * (first / (1.0 - BETA_FIRST**STEP)) / (
+            jnp.sqrt(second / (1.0 - BETA_SECOND**STEP)) + EPSILON
+        )
+
+    for copy in bases[0]:
+        copy.start()
+    mlp_grad = side_by_side(mlp_grad_ref[0], mlp_weight_ref.shape[1])
+    mlp_grad_out[0] = mlp_grad.astype(F32)
     chains = []
     misses = []
     for which in range(together):
         grad = grad_ref[which]
-        width = weight_ref.shape[2]
-        if grad.shape[1] != width:
-            height = weight_ref.shape[1]
-            grad = jnp.concatenate([grad[at:at + height] for at in range(0, grad.shape[0], height)], axis=1)
         grad_out_ref[which] = grad.astype(F32)
         left = left_ref[which]
         right = right_ref[which]
         left_pair = split(left)
         right_pair = split(right)
-        gram = dot_nt(grad, grad)
-        pace = TURN_RATE / (jnp.sqrt(jnp.sum(gram * gram)) + 1e-06)
-        left_base[which] = left + dot_nn(gram.astype(BF), left_pair[0]) * pace
-        right_base[which] = right + dot_tn(grad, dot_nn(grad, right_pair[0]).astype(BF)) * pace
+        set_bases(grad, left, right, left_pair[0], right_pair[0], left_base.at[which], right_base.at[which])
         misses.append(([], []))
         chains.append(renew_chain(right_base.at[which], right_new_ref.at[which], right_rest.at[which], misses[which][1]))
         chains.append(renew_chain(left_base.at[which], left_new_ref.at[which], left_rest.at[which], misses[which][0]))
@@ -200,7 +371,29 @@
                 move_ref.at[which],
             )
         )
+    chains.append(
+        move_chain(
+            mlp_grad, split(mlp_left_ref[0]), split(mlp_right_ref[0]),
+            mlp_weight_ref.at[0], mlp_first_ref.at[0], mlp_second_ref.at[0],
+            mlp_new_ref.at[0], mlp_copy_ref.at[0], mlp_first_new_ref.at[0], mlp_second_new_ref.at[0], mlp_move,
+        )
+    )
     in_step(chains)
+    for copy in bases[0]:
+        copy.wait()
+    poor = jnp.logical_not(jnp.maximum(miss_ref[slot, 0], miss_ref[slot, 1]) < NEAR)
+
+    @pl.when(poor)
+    def _():
+        left = mlp_left_ref[0]
+        right = mlp_right_ref[0]
+        size = left.shape[0]
+        set_bases(mlp_grad, left, right, left.astype(BF), right.astype(BF), left_held, right_held)
+        renew_rows(left_held, left_held, work.at[pl.ds(0, size), pl.ds(0, size)])
+        renew_rows(right_held, right_held, work)
+
+    for copy in bases[1]:
+        copy.start()
     for which in range(together):
         for missed, base, out, rest in zip(
             misses[which], (left_base, right_base), (left_new_ref, right_new_ref), (left_rest, right_rest)
@@ -211,49 +404,75 @@
             def _(base=base, out=out, rest=rest):
                 renew_rows(base.at[which], out.at[which], rest.at[which])
 
-
-def update_stack(grad, skip, together, weight, first, second, left, right):
-    slots, rows, width = weight.shape
-
-    def spec(shape):
-        return pl.BlockSpec((together,) + shape, lambda slot: (slot, 0, 0))
-
-    flat = spec((rows, width))
+    @pl.when(slot == 0)
+    def _():
+        for copy in wide[0]:
+            copy.wait()
+        for copy in wide[1]:
+            copy.start()
+
+    @pl.when(slot == last)
+    def _():
+        for copy in wide[1]:
+            copy.wait()
+
+    for copy in bases[1]:
+        copy.wait()
+
+
+def update(miss, mlp, attn, norms, passed):
+    like = jax.ShapeDtypeStruct
+    slots = mlp[1].shape[0]
+    together = attn[1].shape[0] // slots
+
+    def spec(count, value):
+        return pl.BlockSpec((count,) + value.shape[1:], lambda slot: (slot, 0, 0))
+
+    def made(value):
+        return [like(value.shape, F32)] * 2 + [like(value.shape, BF)] + [like(value.shape, F32)] * 2
+
+    whole = pl.BlockSpec(norms[0].shape, lambda slot: (0, 0))
+    anywhere = pl.BlockSpec(memory_space=pl.ANY)
+    rows, width = attn[1].shape[1:]
+    sides = [pltpu.VMEM((together, rows, rows), F32), pltpu.VMEM((together, width, width), F32)]
+    held = [pltpu.VMEM(value.shape[1:], F32) for value in passed[:2]]
     return pl.pallas_call(
         functools.partial(update_kernel, together),
-        grid=(slots // together,),
-        in_specs=[pl.BlockSpec((together,) + grad.shape[1:], lambda slot: (skip // together + slot, 0, 0))]
-        + [flat] * 3 + [spec((rows, rows)), spec((width, width))],
-        out_specs=[flat] * 5 + [spec((rows, rows)), spec((width, width))],
-        out_shape=[
-            jax.ShapeDtypeStruct(weight.shape, F32),
-            jax.ShapeDtypeStruct(weight.shape, F32),
-            jax.ShapeDtypeStruct(weight.shape, BF),
-            jax.ShapeDtypeStruct(weight.shape, F32),
-            jax.ShapeDtypeStruct(weight.shape, F32),
-            jax.ShapeDtypeStruct(left.shape, F32),
-            jax.ShapeDtypeStruct(right.shape, F32),
-        ],
-        scratch_shapes=[
-            pltpu.VMEM((together, rows, rows), F32),
-            pltpu.VMEM((together, width, width), F32),
-            pltpu.VMEM((together, rows, rows), F32),
-            pltpu.VMEM((together, width, width), F32),
-            pltpu.VMEM((together, rows, width), BF),
-        ],
-        compiler_params=pltpu.CompilerParams(vmem_limit_bytes=60 * 1024 * 1024),
-        name="rotated_update_%d" % width,
-    )(grad, weight, first, second, left, right)
-
-
-MESH = pl.DeviceIdType.MESH
+        grid=(slots,),
+        in_specs=[pl.BlockSpec(memory_space=pltpu.SMEM)]
+        + [spec(1, value) for value in mlp]
+        + [spec(together, value) for value in attn]
+        + [whole] * 4
+        + [anywhere] * 4,
+        out_specs=[spec(1, mlp[1])] * 5
+        + [spec(together, attn[1])] * 5
+        + [spec(together, attn[4]), spec(together, attn[5])]
+        + [whole] * 4
+        + [anywhere] * 4,
+        out_shape=made(mlp[1])
+        + made(attn[1])
+        + [like(attn[4].shape, F32), like(attn[5].shape, F32)]
+        + [like(norms[0].shape, F32)] * 4
+        + [like(value.shape, value.dtype) for value in passed],
+        scratch_shapes=[pltpu.VMEM(mlp[1].shape[1:], BF)]
+        + sides * 2
+        + [pltpu.VMEM((together, rows, width), BF)]
+        + held
+        + [held[1]]
+        + [pltpu.VMEM(value.shape, value.dtype) for value in passed[2:]]
+        + [pltpu.SemaphoreType.DMA((len(passed),)), pltpu.SemaphoreType.DMA((len(passed),))],
+        compiler_params=pltpu.CompilerParams(vmem_limit_bytes=62 * 1024 * 1024),
+        name="update",
+    )(miss, *mlp, *attn, *norms, *passed)
+
+
 P_SIZE = 197
 NBR = 8
 HEAD = 64
 ROWS = 208
 FAR = 200
 CHUNK = 256
-RADIX = 4
+LANES = 128
 PARTS = 3
 
 
@@ -286,19 +505,13 @@
     return value * share, share + value * bell * (1.0 / math.sqrt(2.0 * math.pi))
 
 
-def remote(src, dst, send, recv, device):
-    return pltpu.make_async_remote_copy(
-        src_ref=src, dst_ref=dst, send_sem=send, recv_sem=recv, device_id=device, device_id_type=MESH
-    )
-
-
 def block_kernel(
     chips, images,
     index_ref, valid_ref,
     tokens_ref, cotangent_ref, queue_ref, norms_ref, attn_own, mlp_own,
-    out_ref, input_grad_ref, done, norm_out,
+    out_ref, input_grad_ref, whole, partial, norm_out,
     attn_ref, mlp_ref,
-    asked, parts_out, given, far_f,
+    asked, parts_out, given, far_f, far_key, far_value,
     wide, tokens_f, normed, normal_one, scale_one, query, key, value, probs, mixed,
     middle, normal_two, scale_two, normed_two, cot_low, made,
     mlp_mine, mlp_away, square, both_out, both_grad,
@@ -313,9 +526,10 @@
     width = tokens_ref.shape[1]
     depth = queue_ref.shape[0]
     picks = images * NBR
+    group = LANES // picks
     pairs = width // (2 * HEAD)
     bits = chips.bit_length() - 1
-    height = done.shape[1]
+    height = whole.shape[1]
     grad_two = tokens_f
     grad_query, grad_key, grad_value, grad_mid_low = query, key, value, normed_two
 
@@ -329,11 +543,11 @@
         return carry
 
     lax.fori_loop(1, chips, greet, 0)
-    pick_row = lax.broadcasted_iota(jnp.int32, (picks, depth), 0)
-    wanted = jnp.zeros((picks, depth), jnp.int32)
+    pick_lane = lax.broadcasted_iota(jnp.int32, (8, LANES), 1)
+    wanted = jnp.full((8, LANES), -1, jnp.int32)
     for pick in range(picks):
         wanted = jnp.where(
-            pick_row == pick, index_ref[core * images + pick // NBR, pick % NBR], wanted
+            pick_lane % picks == pick, index_ref[core * images + pick // NBR, pick % NBR], wanted
         )
     asked[0] = wanted
     attn_ref[:, core] = attn_own[...].astype(BF)
@@ -373,24 +587,35 @@
                     start = (which * images + image) * P_SIZE
                     target[image * ROWS:(image + 1) * ROWS, :] = source[start:start + ROWS, :]
 
+    places = lax.broadcasted_iota(jnp.int32, (depth, LANES), 0) + me * depth
+    lane_group = lax.broadcasted_iota(jnp.int32, (1, LANES), 1) // picks
+
+    def answer(turn, carry):
+        wish = jnp.zeros((1, LANES), jnp.int32)
+        for step in range(group):
+            hop = turn * group + step
+
+            @pl.when(hop > 0)
+            def _(hop=hop):
+                ask(hop).wait_recv()
+
+            wish = jnp.where(lane_group == step, asked[hop][:1, :], wish)
+        chooser = jnp.where(wish == places, 1.0, 0.0).astype(BF)
+        picked = dot_tn(chooser, queue_ref[...]).astype(BF)
+        parts_out[pl.ds(turn * group, group)] = picked.reshape(group, picks, width)
+        for step in range(group):
+            hop = turn * group + step
+
+            @pl.when(hop > 0)
+            def _(hop=hop):
+                give(hop).start()
+
+        return carry
+
     wide[:count, :] = tokens_ref[...].astype(F32)
     wide[count:, :] = jnp.zeros((wide.shape[0] - count, width), F32)
     spread(wide, tokens_f)
-
-    places = lax.broadcasted_iota(jnp.int32, (picks, depth), 1) + me * depth
-
-    def choose(wish):
-        chooser = jnp.where(wish == places, 1.0, 0.0).astype(BF)
-        return dot_nn(chooser, queue_ref[...]).astype(BF)
-
-    def answer(hop, carry):
-        ask(hop).wait_recv()
-        parts_out[hop] = choose(asked[hop])
-        give(hop).start()
-        return carry
-
-    lax.fori_loop(1, chips, answer, 0)
-    given[0] = choose(wanted)
+    lax.fori_loop(0, chips // group, answer, 0)
     wide[:count, :] = cotangent_ref[...].astype(F32)
     spread(wide, made)
     own_row = lax.broadcasted_iota(jnp.int32, (ROWS, 1), 0) < P_SIZE
@@ -404,6 +629,9 @@
 
     def place_of(image):
         return pl.ds(pl.multiple_of(image * ROWS, ROWS), ROWS)
+
+    def weight(slot):
+        return attn_ref[slot].reshape(width, width)
 
     def step_norm(image, carry):
         here = place_of(image)
@@ -415,28 +643,39 @@
         return carry
 
     lax.fori_loop(0, images, step_norm, 0)
+    swaps[0].wait_recv()
+
+    def step_own(image, carry):
+        here = place_of(image)
+        low = made[here, :].astype(BF)
+        query[here, :] = dot_nt(low, weight(0)).astype(BF)
+        middle[here, :] = dot_nt(low, weight(1))
+        normal_two[here, :] = dot_nt(low, weight(2))
+        return carry
+
+    lax.fori_loop(0, images, step_own, 0)
 
     def collect(hop, sums):
         give(hop).wait_recv()
         return sums + given[hop].astype(F32)
 
-    far_f[...] = lax.fori_loop(1, chips, collect, given[0].astype(F32))
-    for swap in swaps:
-        swap.wait_recv()
-
-    def weight(slot):
-        return attn_ref[slot].reshape(width, width)
+    far_f[...] = lax.fori_loop(1, chips, collect, parts_out[0].astype(F32))
+    far_low = far_f[...].astype(BF)
+    far_key[...] = dot_nt(far_low, weight(1))
+    far_value[...] = dot_nt(far_low, weight(2))
 
     def step_forward(image, carry):
         here = place_of(image)
         x = tokens_f[here, :]
-        far = far_f[pl.ds(pl.multiple_of(image * NBR, NBR), NBR), :]
-        full = jnp.concatenate([made[here, :][:FAR, :], far], axis=0).astype(BF)
-        normed[here, :] = full
-        q = dot_nt(full, weight(0)).astype(BF)
-        k = dot_nt(full, weight(1)).astype(BF)
-        v = dot_nt(full, weight(2)).astype(BF)
-        query[here, :] = q
+        near = pl.ds(pl.multiple_of(image * NBR, NBR), NBR)
+
+        def with_far(own, far):
+            return jnp.concatenate([own[here, :][:FAR, :], far[near, :]], axis=0).astype(BF)
+
+        normed[here, :] = with_far(made, far_f)
+        q = query[here, :]
+        k = with_far(middle, far_key)
+        v = with_far(normal_two, far_value)
         key[here, :] = k
         value[here, :] = v
         bias = jnp.where(key_lane < P_SIZE, 0.0, -1e30)
@@ -579,10 +818,11 @@
             send(part, sent.at[part, slot], recv.at[part, slot], (step_s.at[part, at], step_r.at[part, at]), (mate, core))
             arrived(part)
             sums = sent[part, slot, :].astype(F32) + recv[part, slot, :].astype(F32)
-        done[part, held, :] = sums.astype(BF)
+        done = whole.at[part]
+        done[held, :] = sums.astype(BF)
         for hop in range(1, RADIX):
             send(
-                part, done.at[part, held], done.at[part, held],
+                part, done.at[held], done.at[held],
                 (spread_s.at[part, hop - 1], spread_r.at[part, hop - 1]), (peers[second](hop), core),
             )
 
@@ -590,13 +830,15 @@
         arrived(part)
         axis = plan[part][0]
         held = rows(digits[axis] * quarter, quarter)
+        done = whole.at[part]
         for hop in range(1, RADIX):
             send(
-                part, done.at[part, held], done.at[part, held],
+                part, done.at[held], done.at[held],
                 (spread_s.at[part, RADIX - 2 + hop], spread_r.at[part, RADIX - 2 + hop]),
                 (peers[axis](hop), core),
             )
 
+    swaps[1].wait_recv()
     step_mlp(other, mlp_away)
     for part in range(2):
         copy_blocks(first_send, mlp_away, part)
@@ -661,10 +903,8 @@
         )
         return carry
 
-    lax.fori_loop(0, images // 2, step_backward, 0)
-    for part in range(2):
-        reduce_two(part)
-    lax.fori_loop(images // 2, images, step_backward, 0)
+    lax.fori_loop(0, images, step_backward, 0)
+    reduce_two(0)
 
     def norm_send(src, dst, place, device):
         copy = remote(src, dst, norm_s.at[place], norm_r.at[place], device)
@@ -690,9 +930,10 @@
         first_send[2, place, :] = square[rows(other * tall, tall), :].astype(BF)
         total[2, place, :] = square[rows(core * tall, tall), :]
     begin(2)
-    for part in range(2):
-        spread_one(part)
+    reduce_two(1)
+    spread_one(0)
     reduce_one(2)
+    spread_one(1)
 
     norm_wait[0].wait_recv()
     norm_sum[...] = norm_pair[0] + norm_pair[1]
@@ -713,7 +954,6 @@
         norm_send(norm_slots.at[1, hi], norm_slots.at[1, hi], RADIX - 1 + hop, (peers[1](hop), core))
         for hop in range(1, RADIX)
     ]
-    spread_one(2)
 
     for join in joins:
         join.wait_recv()
@@ -735,8 +975,12 @@
         norm_sum[...] = norm_slots[2 + turn, 0] + norm_slots[2 + turn, 1]
     norm_out[...] = norm_sum[...]
 
-    spread_two(2)
-    for part in range(PARTS):
+    arrived(2)
+    sums = total[2, rows(lo * quarter + hi * shard, shard), :]
+    for hop in range(1, RADIX):
+        sums = sums + recv[2, pl.ds((RADIX - 1) * quarter + (hop - 1) * shard, shard), :].astype(F32)
+    partial[...] = sums
+    for part in range(2):
         arrived(part)
     for one in pending + joins + swaps:
         one.wait_send()
@@ -772,19 +1016,22 @@
     return pl.pallas_call(
         functools.partial(block_kernel, chips, images),
         in_specs=[smem] * 2 + [vmem] * 6,
-        out_specs=[vmem] * 4,
+        out_specs=[vmem] * 5,
         out_shape=[
             jax.ShapeDtypeStruct((count, width), BF),
             jax.ShapeDtypeStruct((count, width), F32),
-            jax.ShapeDtypeStruct((PARTS, height, width), BF),
+            jax.ShapeDtypeStruct((2, height, width), BF),
+            jax.ShapeDtypeStruct((shard, width), F32),
             jax.ShapeDtypeStruct(norms.shape, F32),
         ],
         scratch_shapes=[
             pltpu.VMEM((attn.shape[0], cores) + attn.shape[1:], BF),
             pltpu.VMEM((mlp.shape[0], cores) + mlp.shape[1:], BF),
-            pltpu.VMEM((chips, picks, queue.shape[0]), jnp.int32),
+            pltpu.VMEM((chips, 8, LANES), jnp.int32),
             pltpu.VMEM((chips, picks, width), BF),
             pltpu.VMEM((chips, picks, width), BF),
+            pltpu.VMEM((picks, width), F32),
+            pltpu.VMEM((picks, width), F32),
             pltpu.VMEM((picks, width), F32),
             pltpu.VMEM((padded, width), F32),
             flat_f, flat_low, flat_f, column, flat_low, flat_low, flat_low,
@@ -819,9 +1066,6 @@
     )(nbr_index, nbr_valid, tokens, cotangent, queue, norms, attn, mlp)
 
 
-RATE_NORM = 0.6
-
-
 def body(
     chips,
     tokens,
@@ -847,27 +1091,16 @@
         return value.transpose(0, 2, 1)
 
     attn_own = flip(attn_weight)
-    block_out, input_grad, summed, norm_grad = block(
+    block_out, input_grad, summed, partial, norm_grad = block(
         chips, nbr_index, nbr_valid, tokens, cotangent, queue, norm_params, attn_own, mlp_weight
     )
-    norm_first_new = BETA_FIRST * norm_first + (1.0 - BETA_FIRST) * norm_grad
-    norm_second_new = BETA_SECOND * norm_second + (1.0 - BETA_SECOND) * norm_grad * norm_grad
-    norm_new = norm_params - RATE_NORM * (norm_first_new / (1.0 - BETA_FIRST**STEP)) / (
-        jnp.sqrt(norm_second_new / (1.0 - BETA_SECOND**STEP)) + EPSILON
-    )
-    slots, rows, width = attn_own.shape
+    left_made, right_made, miss, attn_summed = turn_mlp(chips, summed, mlp_left, mlp_right, partial)
     (
         mlp_grad,
         mlp_new,
         mlp_copy,
         mlp_first_new,
         mlp_second_new,
-        mlp_left_new,
-        mlp_right_new,
-    ) = update_stack(
-        summed, 0, 1, mlp_weight, mlp_first, mlp_second, mlp_left, mlp_right
-    )
-    (
         attn_grad,
         attn_new,
         attn_copy,
@@ -875,15 +1108,27 @@
         attn_second_new,
         attn_right_new,
         attn_left_new,
-    ) = update_stack(
-        summed.reshape(-1, rows, width),
-        2 * slots,
-        2,
-        attn_own,
-        flip(attn_first),
-        flip(attn_second),
-        attn_right,
-        attn_left,
+        norm_grad,
+        norm_new,
+        norm_first_new,
+        norm_second_new,
+        mlp_left_new,
+        mlp_right_new,
+        block_out,
+        input_grad,
+    ) = update(
+        miss,
+        (summed, mlp_weight, mlp_first, mlp_second, mlp_left, mlp_right),
+        (
+            attn_summed.reshape(attn_own.shape),
+            attn_own,
+            flip(attn_first),
+            flip(attn_second),
+            attn_right,
+            attn_left,
+        ),
+        (norm_grad, norm_params, norm_first, norm_second),
+        (left_made, right_made, block_out, input_grad),
     )
     return (
         block_out,

time: 183 us -> 173 us (0.945)
  Pallas kernels: 176 us -> 170 us
  local copies, waits for them, and re-layouts: 3.21 us -> 0 us
    pallas_call x1, Pallas kernels: 103 us -> 88 us  [block(): pl.pallas_call(functools.partial(block_kernel, chips, images), in_specs=[...]
    pallas_call x2, Pallas kernels: 72.8 us -> 81.7 us  [the longest x1 43.1 us: turn_mlp(): pl.pallas_call(functools.partial(turn_mlp_kernel, chips), in_specs=[vmem]...]
    unnamed x15 -> x0, local copies, waits for them, and re-layouts: 3.21 us -> none
where the time goes in v2:
time: 173 us; the launch traced here: 171 us
  Pallas kernels  170 us (98%)
    pallas_call x1, Pallas kernels, block(): pl.pallas_call(functools.partial(block_kernel, chips, images), in_specs=[...  88 us
    pallas_call x1, Pallas kernels, turn_mlp(): pl.pallas_call(functools.partial(turn_mlp_kernel, chips), in_specs=[vmem]...  43.1 us
    pallas_call x1, Pallas kernels, update(): pl.pallas_call(functools.partial(update_kernel, together), grid=(slots,),...  38.6 us

profile of v2, /device:TPU:0, one launch (start us, length us, event | category | flops | bytes accessed | tf_op | source)
XLA Modules:
  0.0 170.6 jit_solution(11799209604129481488)
XLA Ops:
  0.7 88.0 %block_both_ways.1 = (bf16[1576,384]{1,0:T(8,128)(2,1)}, f32[1576,384]{1,0:T(8,128)}, bf16[2,768,384]{2,1,0:T(8,128)(2,1)}, f32[48,384]{1,0:T(8,128)}, f32[4,384]{1,0:T(4,128)}) custom-call(s32[8,8]{1,0:T(8,128)} %index_ref.1, s32[8,8]{1,0:T(8,128)} %valid_ref.1, bf16[1576,384]{1,0:T(8,128)(2,1)} %tokens_ref.1, bf16[1576,384]{1,0:T(8,128)(2,1)} %cotangent_ref.1, ...), custom_call_target="tpu_custom_call" | custom-call | tf_op jit(solution)/shard_map/block_both_ways/pallas_call | solution.py:1016
  88.7 43.1 %turn_mlp.1 = (f32[2,384,384]{2,1,0:T(8,128)}, f32[2,768,768]{2,1,0:T(8,128)}, f32[2,2]{1,0:T(2,128)}, bf16[768,384]{1,0:T(8,128)(2,1)}) custom-call(bf16[2,768,384]{2,1,0:T(8,128)(2,1)} %get-tuple-element.49.grad_ref.mlp_grad_ref, f32[2,384,384]{2,1,0:T(8,128)} %mlp_left_ref.1, f32[2,768,768]{2,1,0:T(8,128)} %mlp_right_ref.1, ...), custom_call_target="tpu_custom_call" | custom-call | tf_op jit(solution)/shard_map/turn_mlp/pallas_call | solution.py:282
  131.8 38.6 %update.1 = (f32[2,384,768]{2,1,0:T(8,128)}, f32[2,384,768]{2,1,0:T(8,128)}, bf16[2,384,768]{2,1,0:T(8,128)(2,1)}, f32[2,384,768]{2,1,0:T(8,128)}, f32[2,384,768...) custom-call(f32[2,2]{1,0:T(2,128)} %get-tuple-element.51.miss_ref, ...), custom_call_target="tpu_custom_call" | custom-call | tf_op jit(solution)/shard_map/update/pallas_call | solution.py:439
